TPU v7x, 512 devices: a whole 4x8x8 slice. The times are simulated.
512 devices in a mesh: row: 16 (over z, core), col: 32 (over y, x).
Axes of the slice: x: 4, y: 8, z: 8, core: 2. Of those that a mesh axis runs over, the one named last changes fastest.
Arguments:
- band_sites: float32 [2, 512], P(None, 'row'), may hold values from 0 to 1
- test_sites: float32 [2, 4096], P(None, 'col'), may hold values from 0 to 1
- band_factor: float32 [512, 512], P('row', 'col'), as said below
- prior_factor: float32 [512, 8192], P('row', 'col'), may hold values from -0.0625 to 0.0625
- prior_solution: float32 [8192, 4096], P('col', 'row'), may hold values from -6 to 6
- prior_covariance: float32 [4096, 4096], P('row', 'col'), may hold values from -4 to 4
Outputs:
- band_solution: float32 [512, 4096], P('row', 'col')
- covariance: float32 [4096, 4096], P('row', 'col')
Inputs may be any that keep to these rules, and one draw needn't show every extreme that they name: band_factor is lower triangular with diagonal entries in 1 to 2 and small entries below it.
All inputs are finite; a program needn't handle non-finite values.
Results may differ from a plain program's by a relative error of at most 0.00011.
Values sent between devices are 32-bit elements; how exact they have to be, the bound alone decides.
A program may use at most 64 MiB of HBM per device.

v0:
```python
import jax
import jax.numpy as jnp
from jax import lax
from jax.sharding import PartitionSpec as P

length_scale = 0.3


def copy_for_each(array, axis):
    devices = lax.axis_size(axis)
    return lax.all_to_all(
        jnp.broadcast_to(array[None], (devices, *array.shape)), axis, 0, 0, tiled=True
    )


def joined_along(blocks, dim):
    blocks = jnp.moveaxis(blocks, 0, dim)
    lengths = blocks.shape
    return blocks.reshape(*lengths[:dim], lengths[dim] * lengths[dim + 1], *lengths[dim + 2 :])


def gathered_copies(array, axis, dim):
    blocks = copy_for_each(array, axis)
    return joined_along(blocks, dim)


def cut_along(array, dim, devices):
    before, after = (array.shape[:dim], array.shape[dim + 1 :])
    return jnp.moveaxis(array.reshape(*before, devices, -1, *after), dim, 0)


def sum_at_owner(array, axis, dim):
    devices = lax.axis_size(axis)
    blocks = lax.all_to_all(cut_along(array, dim, devices), axis, 0, 0, tiled=True)
    return jnp.sum(blocks, axis=0)


def matern(band_sites, test_sites):
    delta_x = band_sites[0][:, None] - test_sites[0][None, :]
    delta_y = band_sites[1][:, None] - test_sites[1][None, :]
    scaled = jnp.sqrt(delta_x * delta_x + delta_y * delta_y + 1e-06) * (3.0**0.5 / length_scale)
    return (1.0 + scaled) * jnp.exp(-scaled)


def local(band_sites, test_sites, band_factor, prior_factor, prior_solution, prior_covariance):
    tile_rows = band_factor.shape[0]
    test_cols = test_sites.shape[1]
    row_count = lax.axis_size("row")
    my_row = lax.axis_index("row")
    cross = matern(band_sites, test_sites)
    all_rows = jnp.dot(
        gathered_copies(prior_factor, "row", 0),
        prior_solution,
        precision=lax.Precision.HIGHEST,
        preferred_element_type=jnp.float32,
    )
    own_rows = lax.all_to_all(all_rows, "row", split_axis=0, concat_axis=1, tiled=True)
    update = sum_at_owner(own_rows, "col", 1)
    remaining = cross - update
    factor_row = gathered_copies(band_factor, "col", 1)
    whole_rest = gathered_copies(remaining, "row", 0)
    whole_factor = lax.all_gather(factor_row, "row", axis=0, tiled=True)
    whole_solved = lax.linalg.triangular_solve(whole_factor, whole_rest, left_side=True, lower=True)
    collected = whole_solved.reshape(row_count, tile_rows, test_cols)
    band_solution = lax.dynamic_index_in_dim(collected, my_row, 0, keepdims=False)
    band_rows = gathered_copies(band_solution, "col", 1)
    gram_sum = sum_at_owner(
        lax.dot_general(
            band_rows,
            band_solution,
            (((0,), (0,)), ((), ())),
            precision=lax.Precision.HIGHEST,
            preferred_element_type=jnp.float32,
        ),
        "row",
        0,
    )
    return (band_solution, prior_covariance - gram_sum)


def solution(mesh):
    placed = (
        P(None, "row"),
        P(None, "col"),
        P("row", "col"),
        P("row", "col"),
        P("col", "row"),
        P("row", "col"),
    )
    return jax.shard_map(
        local,
        mesh=mesh,
        in_specs=placed,
        out_specs=(P("row", "col"), P("row", "col")),
        check_vma=False,
    )
```

profile of v0, /device:TPU:1, one launch (start us, length us, event | category | flops | bytes accessed | tf_op | source)
XLA Modules:
  0.0 250.7 jit_solution(8510704204198019429)
XLA Ops:
  7.2 0.8 broadcast_bitcast_fusion
  8.1 19.1 %all_to_all.43 = f32[32,1,512]{2,1,0:T(1,128)S(1)} all-to-all(f32[32,1,512]{2,1,0:T(1,128)S(1)} %reshape.138), channel_id=1, replica_groups=mesh['row'=16,'col'=32] {'col'}, dimensions={0} | all-to-all | bytes 131072 | tf_op jit(solution)/shard_map/all_to_all | solution.py:11
  27.2 1.6 broadcast_in_dim.9
  28.9 12.4 %all-to-all-start.1 = ((f32[16,32,256]{2,1,0:T(8,128)}), f32[16,32,256]{2,1,0:T(8,128)S(1)}, u32[]{:S(2)}, u32[]{:S(2)}) async-start(f32[16,32,256]{2,1,0:T(8,128)} %broadcast_in_dim.9), calls=%async_computation.1 | async-start | bytes 1048576 | tf_op jit(solution)/shard_map/all_to_all | solution.py:11
  41.9 0.8 reduce
  42.8 0.7 copy.12
  43.6 15.1 %all-to-all-done.1 = f32[16,32,256]{2,1,0:T(8,128)S(1)} async-done(((f32[16,32,256]{2,1,0:T(8,128)}), f32[16,32,256]{2,1,0:T(8,128)S(1)}, u32[]{:S(2)}, u32[]{:S(2)}) %all-to-all-start.1) | async-done | bytes 524320 | tf_op jit(solution)/shard_map/all_to_all | solution.py:11
  59.2 21.1 %all_to_all.44 = f32[16,32,256]{2,1,0:T(8,128)S(1)} all-to-all(f32[16,32,256]{2,1,0:T(8,128)S(1)} %fusion.4), channel_id=1, replica_groups=mesh['row'=16,'col'=32] {'row'}, dimensions={0} | all-to-all | bytes 1048576 | tf_op jit(solution)/shard_map/all_to_all | solution.py:57
  80.7 1.1 copy.14
  81.8 4.0 %all-to-all-start.3 = ((f32[32,32,128]{2,1,0:T(8,128)}), f32[32,32,128]{2,1,0:T(8,128)S(1)}, u32[]{:S(2)}, u32[]{:S(2)}) async-start(f32[32,32,128]{2,1,0:T(8,128)} %copy.14), calls=%async_computation.3 | async-start | bytes 1048576 | tf_op jit(solution)/shard_map/all_to_all | solution.py:34
  85.9 1.3 fusion
  87.3 15.3 %all-to-all-done.3 = f32[32,32,128]{2,1,0:T(8,128)S(1)} async-done(((f32[32,32,128]{2,1,0:T(8,128)}), f32[32,32,128]{2,1,0:T(8,128)S(1)}, u32[]{:S(2)}, u32[]{:S(2)}) %all-to-all-start.3) | async-done | bytes 524320 | tf_op jit(solution)/shard_map/all_to_all | solution.py:34
  102.8 0.7 broadcast_in_dim.10
  103.5 5.6 %all-to-all-start.4 = ((f32[16,32,128]{2,1,0:T(8,128)}), f32[16,32,128]{2,1,0:T(8,128)S(1)}, u32[]{:S(2)}, u32[]{:S(2)}) async-start(f32[16,32,128]{2,1,0:T(8,128)} %broadcast_in_dim.10), calls=%async_computation.4 | async-start | bytes 524288 | tf_op jit(solution)/shard_map/all_to_all | solution.py:11
  109.1 7.7 %while.1 = (s32[]{:T(128)}, f32[512,512]{1,0:T(8,128)S(1)}, s32[4,2]{0,1:T(2,128)S(1)}, f32[4,128,128]{2,1,0:T(8,128)S(1)}, s32[]{:T(128)}) while((s32[]{:T(128)}, f32[512,512]{1,0:T(8,128)S(1)}, s32[4,2]{0,1:T(2,128)S(1)}, f32[4,128,128]{2,1,0:T(8,128)S(1)}, s32[]{:T(128)}) %tuple.29), condition=%wide.while_cond, body=%wide.while_body.sunk | while | flops 2 | bytes 131189 | solution.py:63
  109.7 1.3 bitcast_dynamic-update-slice_fusion.2
  111.6 1.3 bitcast_dynamic-update-slice_fusion.2
  113.5 1.3 bitcast_dynamic-update-slice_fusion.2
  115.5 1.3 bitcast_dynamic-update-slice_fusion.2
  116.8 39.3 %custom-call.3 = f32[4,128,128]{1,2,0:T(8,128)S(1)} custom-call(f32[4,128,128]{2,1,0:T(8,128)S(1)} %get-tuple-element.9), custom_call_target="InvertDiagBlocksLowerTriangular" | custom-call | tf_op jit(solution)/shard_map/triangular_solve | solution.py:63
  158.2 20.9 %all_to_all.45 = f32[32,32,128]{2,1,0:T(8,128)S(1)} all-to-all(f32[32,32,128]{2,1,0:T(8,128)S(1)} %broadcast_in_dim.11), channel_id=1, replica_groups=mesh['row'=16,'col'=32] {'col'}, dimensions={0} | all-to-all | bytes 1048576 | tf_op jit(solution)/shard_map/all_to_all | solution.py:11
  179.2 3.4 %fusion.1 = f32[16,256,128]{2,1,0:T(8,128)S(1)} fusion(f32[4,16,8,256]{3,2,1,0:T(8,128)S(1)} %bitcast.70, f32[16,32,128]{2,1,0:T(8,128)S(1)} %bitcast.73, s32[]{:T(128)S(6)} %select_n.4), kind=kOutput, calls=%fused_computation.8 | convolution fusion | flops 201326592 | bytes 2637828 | tf_op jit(solution)/shard_map/dot_general | solution.py:68
  182.6 59.7 %all_to_all.46 = f32[16,256,128]{2,1,0:T(8,128)S(1)} all-to-all(f32[16,256,128]{2,1,0:T(8,128)S(1)} %fusion.1), channel_id=1, replica_groups=mesh['row'=16,'col'=32] {'row'}, dimensions={0} | all-to-all | bytes 4194304 | tf_op jit(solution)/shard_map/all_to_all | solution.py:34
  242.4 0.8 copy-done.1
  (48 shorter events, 7.2 us)
Async XLA Ops:
  7.2 51.5 %copy-start = (f32[256,256]{1,0:T(8,128)S(1)}, f32[256,256]{1,0:T(8,128)}, u32[]{:S(2)}) copy-start(f32[256,256]{1,0:T(8,128)} %param.10) | copy-start | bytes 786436
  28.9 29.8 %all-to-all-start.1 = ((f32[16,32,256]{2,1,0:T(8,128)}), f32[16,32,256]{2,1,0:T(8,128)S(1)}, u32[]{:S(2)}, u32[]{:S(2)}) async-start(f32[16,32,256]{2,1,0:T(8,128)} %broadcast_in_dim.9), calls=%async_computation.1 | async-start | bytes 1048576 | tf_op jit(solution)/shard_map/all_to_all | solution.py:11
  41.3 44.6 %all-gather.2.cloned.1.call-start = ((), (), s32[]{:S(2)}) async-start(), calls=%async_computation.7 | async-start | bytes 1114112 | tf_op jit(solution)/shard_map/all_gather | solution.py:62
  80.3 5.5 %copy-start.3 = (f32[2,32]{1,0:T(2,128)S(1)}, f32[2,32]{1,0:T(2,128)}, u32[]{:S(2)}) copy-start(f32[2,32]{1,0:T(2,128)} %param.6) | copy-start | bytes 772
  80.3 5.5 %copy-start.4 = (f32[2,128]{1,0:T(2,128)S(1)}, f32[2,128]{1,0:T(2,128)}, u32[]{:S(2)}) copy-start(f32[2,128]{1,0:T(2,128)} %param.7) | copy-start | bytes 3076
  81.8 20.8 %all-to-all-start.3 = ((f32[32,32,128]{2,1,0:T(8,128)}), f32[32,32,128]{2,1,0:T(8,128)S(1)}, u32[]{:S(2)}, u32[]{:S(2)}) async-start(f32[32,32,128]{2,1,0:T(8,128)} %copy.14), calls=%async_computation.3 | async-start | bytes 1048576 | tf_op jit(solution)/shard_map/all_to_all | solution.py:34
  103.5 52.6 %all-to-all-start.4 = ((f32[16,32,128]{2,1,0:T(8,128)}), f32[16,32,128]{2,1,0:T(8,128)S(1)}, u32[]{:S(2)}, u32[]{:S(2)}) async-start(f32[16,32,128]{2,1,0:T(8,128)} %broadcast_in_dim.10), calls=%async_computation.4 | async-start | bytes 524288 | tf_op jit(solution)/shard_map/all_to_all | solution.py:11
  158.2 24.5 %copy-start.2 = (f32[32,128]{1,0:T(8,128)}, f32[32,128]{1,0:T(8,128)S(1)}, u32[]{:S(2)}) copy-start(f32[32,128]{1,0:T(8,128)S(1)} %dynamic-slice_bitcast_fusion) | copy-start | bytes 49156
  242.3 0.9 copy-start.1
Sparse Core Ops, SparseCore 0:
  44.8 39.0 all-gather.1
where the time goes:
time: 251 us
  blocking collectives  121 us (48%)
  other arithmetic  42.4 us (17%)
  waiting for transfers between devices  30.5 us (12%)
  starting transfers between devices  22 us (9%)
  local copies, waits for them, and re-layouts  14.7 us (6%)
  between operations  14.3 us (6%)
  matrix products  5.94 us (2%)
    all_to_all x1, blocking collectives, sum_at_owner(): lax.all_to_all(cut_along(array, dim, devices), axis, 0, 0, tiled=True)  59.7 us
    another operation x4, other arithmetic, local(): lax.linalg.triangular_solve(whole_factor, whole_rest, left_side=True, low...  40.7 us
    all_to_all x2, blocking collectives, copy_for_each(): lax.all_to_all(jnp.broadcast_to(array[None], (devices, *array.shape)), ax...  40 us
    all_to_all x1, blocking collectives, local(): lax.all_to_all(all_rows, 'row', split_axis=0, concat_axis=1, tiled=True)  21.1 us
    all_to_all x2, starting transfers between devices, copy_for_each(): lax.all_to_all(jnp.broadcast_to(array[None], (devices, *array.shape)), ax...  18 us
    all_to_all x1, waiting for transfers between devices, sum_at_owner(): lax.all_to_all(cut_along(array, dim, devices), axis, 0, 0, tiled=True)  15.3 us
    all_to_all x2, waiting for transfers between devices, copy_for_each(): lax.all_to_all(jnp.broadcast_to(array[None], (devices, *array.shape)), ax...  15.1 us
    another operation x12, local copies, waits for them, and re-layouts  7.62 us
  transfers between devices with their start and end apart: 4, of which 2 were waited for; matrix products, arithmetic and copies ran while one was open for 21% of the time, Pallas kernels for 0%

commit v1 on v0

v1 whole, which is shorter than its diff:
```python
import jax
import jax.numpy as jnp
from jax import lax
from jax.experimental import pallas as pl
from jax.experimental.pallas import tpu as pltpu
from jax.sharding import PartitionSpec as P

length_scale = 0.3
MESH = pl.DeviceIdType.MESH
F32 = jnp.float32
BF16 = jnp.bfloat16
NZ, NY, NX = 8, 8, 4


def halves(value):
    high = value.astype(BF16)
    return high, (value - high.astype(F32)).astype(BF16)


def dot(a, b, dims):
    return lax.dot_general(a, b, (dims, ((), ())), preferred_element_type=F32)


def dot3(a, b, dims=((1,), (0,))):
    (ah, al), (bh, bl) = a, b
    return dot(ah, bh, dims) + (dot(ah, bl, dims) + dot(al, bh, dims))


def mul(a, b):
    return dot3(halves(a), halves(b))


def upper_inverses(blocks):
    n = 128
    i = lax.broadcasted_iota(jnp.int32, (n, n), 0)
    j = lax.broadcasted_iota(jnp.int32, (n, n), 1)
    done = []
    for u in blocks:
        inv = jnp.where(i == j, 1.0 / jnp.where(i == j, u, 1.0), 0.0)
        down = jnp.sum(inv, axis=1, keepdims=True)
        across = jnp.sum(inv, axis=0, keepdims=True)
        pair = (i // 2 == j // 2) & (i < j)
        done.append(inv - jnp.where(pair, u * down * across, 0.0))
    size = 2
    while size < n:
        part = (i // (2 * size) == j // (2 * size)) & (i // size < j // size)
        left = [halves(x) for x in done]
        mid = [dot3(x, halves(jnp.where(part, u, 0.0))) for x, u in zip(left, blocks)]
        done = [x - dot3(halves(m), xh) for x, m, xh in zip(done, mid, left)]
        size *= 2
    return done


def kernel(
    bs, ts, lf, a, s, pc, v_out, cov_out,
    abuf, sh, sl, pb, xb, ys, yb, cr, sb,
    lzs, lz, lms, lp, lt16, lt, yi, wh, wl,
    own, rr, zb, rcx, rc,
    send, rec, a_rec, ap_rec,
):
    row = lax.axis_index("row")
    col = lax.axis_index("col")
    z, core = row // 2, row % 2
    y, x = col // NX, col % NX
    partner = (2 * z + 1 - core, col)

    def at_z(zz):
        return (2 * zz + core, col)

    def at_y(yy):
        return (row, yy * NX + x)

    def at_x(xx):
        return (row, y * NX + xx)

    def push(src, dst, k, device, recv=None):
        pltpu.make_async_remote_copy(
            src_ref=src,
            dst_ref=dst,
            send_sem=send.at[k],
            recv_sem=rec.at[k] if recv is None else recv,
            device_id=device,
            device_id_type=MESH,
        ).start()

    def await_bytes(ref, sem):
        pltpu.make_async_copy(ref, ref, sem).wait()

    barrier = pltpu.get_barrier_semaphore()
    peers = [partner]
    peers += [at_z((z + d) % NZ) for d in range(1, NZ)]
    peers += [at_y((y + d) % NY) for d in range(1, NY)]
    peers += [at_x((x + d) % NX) for d in range(1, NX)]
    for peer in peers:
        pl.semaphore_signal(barrier, inc=1, device_id=peer, device_id_type=MESH)
    pl.semaphore_wait(barrier, len(peers))

    k_lz, k_lp, k_ly1, k_ly0, k_lx1, k_lx0, k_lq1, k_lq0, k_yi = range(9)
    k_a, k_ap, k_sz, k_sp, k_px, k_uy, k_ry, k_rz, k_cy, k_rx, k_cx, k_cp = range(9, 21)

    place = (
        lax.broadcasted_iota(jnp.int32, (32, 128), 1)
        == lax.broadcasted_iota(jnp.int32, (32, 128), 0) + 32 * (row % 4)
    ).astype(F32)
    tile = lax.dot_general(
        lf[...], place, (((0,), (0,)), ((), ())),
        precision=lax.Precision.HIGHEST, preferred_element_type=F32,
    )
    lzs[...] = tile
    lz[z] = tile
    for d in range(1, NZ):
        push(lzs, lz.at[z], k_lz, at_z((z + d) % NZ))
    push(a, abuf.at[z, core], k_ap, partner, ap_rec.at[z])
    for d in (1, 7, 2, 6, 3, 5, 4):
        push(a, abuf.at[z, core], k_a, at_z((z + d) % NZ), a_rec.at[z])
    abuf[z, core] = a[...]
    sb[z, core, 0:2, 0:32] = bs[...]

    @pl.when(z != y)
    def _():
        push(sb.at[z, core], sb.at[z, core], k_sz, at_z(y))

    sh[...], sl[...] = halves(s[...])

    await_bytes(lz.at[0:7], rec.at[k_lz])
    for q in range(4):
        lms[q] = lz[2 * q] + lz[2 * q + 1]
    push(lms, lp, k_lp, partner)

    root_core = x // 2

    @pl.when(z == y)
    def _():
        await_bytes(sb.at[0:7, 0], rec.at[k_sz])

        @pl.when(core != root_core)
        def _():
            push(sb.at[:, core], sb.at[:, core], k_sp, partner)

    await_bytes(lp, rec.at[k_lp])
    for q in range(4):
        lt16[q] = lms[q] + lp[q]
    lt[core, 0, y, x] = lt16[core]
    lt[core, 1, y, x] = lt16[3 - core]
    for d in range(1, NY):
        push(lt.at[core, 1, y, x], lt.at[core, 1, y, x], k_ly1, at_y((y + d) % NY))

    @pl.when(y < 4)
    def _():
        for d in range(1, NY):
            push(lt.at[core, 0, y, x], lt.at[core, 0, y, x], k_ly0, at_y((y + d) % NY))

    root = (z == y) & (core == root_core)

    @pl.when(root)
    def _():
        await_bytes(sb.at[:, 0], rec.at[k_sp])
        tx, ty = ts[0:1, :], ts[1:2, :]
        for zz in range(NZ):
            for cc in range(2):
                spots = sb[zz, cc].T
                dx = spots[0:32, 0:1] - tx
                dy = spots[0:32, 1:2] - ty
                scaled = jnp.sqrt(dx * dx + dy * dy + 1e-06) * (3.0**0.5 / length_scale)
                cr[zz, cc] = (1.0 + scaled) * jnp.exp(-scaled)

    pair0 = z // 2
    for step, o in enumerate((0, 1, 3, 2)):
        p = (pair0 + o) % 4
        for zz in (2 * p, 2 * p + 1):

            @pl.when(zz != z)
            def _():
                await_bytes(a, a_rec.at[zz])
                push(abuf.at[zz, core], abuf.at[zz, core], k_ap, partner, ap_rec.at[zz])

        for zz in (2 * p, 2 * p + 1):
            await_bytes(a, ap_rec.at[zz])
        rows = abuf[pl.ds(2 * p, 2)].reshape(128, 256)
        pb[p] = dot3(halves(rows), (sh[...], sl[...]))

        @pl.when(root)
        def _():
            lanes = pl.ds(pl.multiple_of(128 * (x % 2), 128), 128)
            pb[p, :, lanes] = pb[p, :, lanes] - cr[pl.ds(2 * p, 2)].reshape(128, 128)

        @pl.when(p != x)
        def _():
            push(pb.at[p], xb.at[x], k_px, at_x(p))

        if step == 1:
            await_bytes(lt.at[0, 1, 0:7, 0], rec.at[k_ly1])

            @pl.when(y < 4)
            def _():
                await_bytes(lt.at[0, 0, 0:3, 0], rec.at[k_ly0])

            @pl.when(y >= 4)
            def _():
                await_bytes(lt.at[0, 0, 0:4, 0], rec.at[k_ly0])

            for d in range(1, NX):
                push(lt.at[core, 1, :, x], lt.at[core, 1, :, x], k_lx1, at_x((x + d) % NX))
                push(lt.at[core, 0, 0:4, x], lt.at[core, 0, 0:4, x], k_lx0, at_x((x + d) % NX))

    xb[x] = pb[x]
    await_bytes(lt.at[0, 1, :, 0:3], rec.at[k_lx1])
    await_bytes(lt.at[0, 0, 0:4, 0:3], rec.at[k_lx0])
    push(lt.at[core, 1], lt.at[core, 1], k_lq1, partner)
    push(lt.at[core, 0, 0:4], lt.at[core, 0, 0:4], k_lq0, partner)

    await_bytes(xb.at[0:3], rec.at[k_px])
    total = (xb[0] + xb[1]) + (xb[2] + xb[3])
    ys[...] = total.reshape(8, 16, 256)
    for d in range(1, NY):
        push(ys.at[(y + d) % NY], yb.at[y], k_uy, at_y((y + d) % NY))
    yb[y] = ys[y]

    q0, q1 = core, 3 - core
    u0 = lt[core, 0, pl.ds(2 * q0, 2)].reshape(128, 128)
    u1 = lt[core, 1, pl.ds(2 * q1, 2)].reshape(128, 128)
    w0, w1 = upper_inverses([u0, u1])
    yi[q0] = w0
    yi[q1] = w1
    push(yi.at[q0], yi.at[q0], k_yi, partner)
    push(yi.at[q1], yi.at[q1], k_yi, partner)

    await_bytes(yb.at[0:7], rec.at[k_uy])
    mine = -(((yb[0] + yb[1]) + (yb[2] + yb[3])) + ((yb[4] + yb[5]) + (yb[6] + yb[7])))
    own[...] = mine
    for d in range(1, NZ):
        push(own, zb.at[z], k_rz, at_z((z + d) % NZ))
    for d in range(1, NY):
        push(own, rr.at[x, y], k_ry, at_y((y + d) % NY))
    zb[z] = mine
    rr[x, y] = mine
    await_bytes(zb.at[0:7], rec.at[k_rz])
    for d in range(1, NY):
        push(zb.at[(y + d) % NY], rcx.at[y], k_cy, at_y((y + d) % NY))
    rcx[y] = zb[y]
    await_bytes(rr.at[0, 0:7], rec.at[k_ry])
    for d in range(1, NX):
        push(rr.at[x], rr.at[x], k_rx, at_x((x + d) % NX))
    await_bytes(rcx.at[0:7], rec.at[k_cy])
    mine_here = root_core == core
    for half in range(2):
        xx = 2 * core + half
        lanes = slice(128 * half, 128 * half + 128)

        @pl.when(xx != x)
        def _():
            push(rcx.at[:, :, lanes], rc.at[x], k_cx, at_x(xx))

        @pl.when(xx == x)
        def _():
            rc[x] = rcx[:, :, lanes]

    await_bytes(yi.at[0:2], rec.at[k_yi])
    await_bytes(lt.at[0, 1], rec.at[k_lq1])
    await_bytes(lt.at[0, 0, 0:4], rec.at[k_lq0])
    where = {0: (0, 0), 3: (0, 1), 1: (1, 0), 2: (1, 1)}

    def block(j, q):
        k, slot = where[q]
        return halves(lt[k, slot, 2 * j : 2 * j + 2].reshape(128, 128))

    w = [yi[q] for q in range(4)]
    ws = [halves(v) for v in w]
    w01 = -dot3(halves(dot3(ws[0], block(0, 1))), ws[1])
    w23 = -dot3(halves(dot3(ws[2], block(2, 3))), ws[3])
    h01, h23 = halves(w01), halves(w23)
    t02 = halves(dot3(ws[0], block(0, 2)) + dot3(h01, block(1, 2)))
    t03 = halves(dot3(ws[0], block(0, 3)) + dot3(h01, block(1, 3)))
    t12 = halves(dot3(ws[1], block(1, 2)))
    t13 = halves(dot3(ws[1], block(1, 3)))
    w02 = -dot3(t02, ws[2])
    w03 = -(dot3(t02, h23) + dot3(t03, ws[3]))
    w12 = -dot3(t12, ws[2])
    w13 = -(dot3(t12, h23) + dot3(t13, ws[3]))
    full = {(0, 0): w[0], (1, 1): w[1], (2, 2): w[2], (3, 3): w[3]}
    full.update({(0, 1): w01, (2, 3): w23, (0, 2): w02, (0, 3): w03, (1, 2): w12, (1, 3): w13})
    for j in range(4):
        for q in range(4):
            here = (slice(128 * q, 128 * q + 128), slice(128 * j, 128 * j + 128))
            if (j, q) in full:
                wh[here], wl[here] = halves(full[j, q].T)
            else:
                wh[here] = jnp.zeros((128, 128), BF16)
                wl[here] = jnp.zeros((128, 128), BF16)

    await_bytes(rr.at[0:3], rec.at[k_rx])
    inverse = (wh[...], wl[...])
    vr = dot3(inverse, halves(rr[...].reshape(512, 256)))

    @pl.when(mine_here)
    def _():
        await_bytes(rc.at[0:3], rec.at[k_cx])
        push(rc, rc, k_cp, partner)

    @pl.when(root_core != core)
    def _():
        await_bytes(rc, rec.at[k_cp])

    vc = dot3(inverse, halves(rc[...].reshape(512, 128)))
    rc_rows = vc.reshape(16, 32, 128)
    cov_out[...] = pc[...] - dot3(halves(vr), halves(vc), ((0,), (0,)))
    xb[0, :, 0:128] = rc_rows[0:4].reshape(128, 128)
    xb[1, :, 0:128] = rc_rows[4:8].reshape(128, 128)
    xb[2, :, 0:128] = rc_rows[8:12].reshape(128, 128)
    xb[3, :, 0:128] = rc_rows[12:16].reshape(128, 128)
    v_out[...] = xb[row // 4, pl.ds(pl.multiple_of(32 * (row % 4), 32), 32), 0:128]

    await_bytes(lz.at[0:7], send.at[k_lz])
    await_bytes(lp, send.at[k_lp])
    await_bytes(lt.at[0, 1, 0:7, 0], send.at[k_ly1])

    @pl.when(y < 4)
    def _():
        await_bytes(lt.at[0, 0, 0:7, 0], send.at[k_ly0])

    await_bytes(lt.at[0, 1, :, 0:3], send.at[k_lx1])
    await_bytes(lt.at[0, 0, 0:4, 0:3], send.at[k_lx0])
    await_bytes(lt.at[0, 1], send.at[k_lq1])
    await_bytes(lt.at[0, 0, 0:4], send.at[k_lq0])
    await_bytes(yi.at[0:2], send.at[k_yi])
    await_bytes(abuf.at[0:7, 0], send.at[k_a])
    await_bytes(abuf.at[:, 0], send.at[k_ap])

    @pl.when(z != y)
    def _():
        await_bytes(sb.at[0, 0], send.at[k_sz])

    @pl.when((z == y) & (core != root_core))
    def _():
        await_bytes(sb.at[:, 0], send.at[k_sp])

    await_bytes(xb.at[0:3], send.at[k_px])
    await_bytes(yb.at[0:7], send.at[k_uy])
    await_bytes(zb.at[0:7], send.at[k_rz])
    await_bytes(rr.at[0, 0:7], send.at[k_ry])
    await_bytes(rcx.at[0:7], send.at[k_cy])
    await_bytes(rr.at[0:3], send.at[k_rx])

    @pl.when(mine_here)
    def _():
        await_bytes(rc.at[0], send.at[k_cx])
        await_bytes(rc, send.at[k_cp])

    @pl.when(root_core != core)
    def _():
        await_bytes(rc.at[0:2], send.at[k_cx])


def local(band_sites, test_sites, band_factor, prior_factor, prior_solution, prior_covariance):
    vmem = pl.BlockSpec(memory_space=pltpu.VMEM)
    scratch = [
        pltpu.VMEM((8, 2, 32, 256), F32),
        pltpu.VMEM((256, 256), BF16),
        pltpu.VMEM((256, 256), BF16),
        pltpu.VMEM((4, 128, 256), F32),
        pltpu.VMEM((4, 128, 256), F32),
        pltpu.VMEM((8, 16, 256), F32),
        pltpu.VMEM((8, 16, 256), F32),
        pltpu.VMEM((8, 2, 32, 128), F32),
        pltpu.VMEM((8, 2, 8, 128), F32),
        pltpu.VMEM((16, 128), F32),
        pltpu.VMEM((8, 16, 128), F32),
        pltpu.VMEM((4, 16, 128), F32),
        pltpu.VMEM((4, 16, 128), F32),
        pltpu.VMEM((4, 16, 128), F32),
        pltpu.VMEM((2, 2, 8, 4, 16, 128), F32),
        pltpu.VMEM((4, 128, 128), F32),
        pltpu.VMEM((512, 512), BF16),
        pltpu.VMEM((512, 512), BF16),
        pltpu.VMEM((16, 256), F32),
        pltpu.VMEM((4, 8, 16, 256), F32),
        pltpu.VMEM((8, 16, 256), F32),
        pltpu.VMEM((8, 16, 256), F32),
        pltpu.VMEM((4, 8, 16, 128), F32),
        pltpu.SemaphoreType.DMA((21,)),
        pltpu.SemaphoreType.DMA((21,)),
        pltpu.SemaphoreType.DMA((8,)),
        pltpu.SemaphoreType.DMA((8,)),
    ]
    return pl.pallas_call(
        kernel,
        out_shape=(
            jax.ShapeDtypeStruct((32, 128), F32),
            jax.ShapeDtypeStruct((256, 128), F32),
        ),
        in_specs=[vmem] * 6,
        out_specs=(vmem, vmem),
        scratch_shapes=scratch,
        compiler_params=pltpu.CompilerParams(
            collective_id=0, has_side_effects=True, vmem_limit_bytes=32 * 1024 * 1024
        ),
    )(band_sites, test_sites, band_factor, prior_factor, prior_solution, prior_covariance)


def solution(mesh):
    placed = (
        P(None, "row"),
        P(None, "col"),
        P("row", "col"),
        P("row", "col"),
        P("col", "row"),
        P("row", "col"),
    )
    return jax.shard_map(
        local,
        mesh=mesh,
        in_specs=placed,
        out_specs=(P("row", "col"), P("row", "col")),
        check_vma=False,
    )
```

time: 251 us -> 72.1 us (0.29)
  blocking collectives: 121 us -> 0 us
  Pallas kernels: 0 us -> 66.5 us
  other arithmetic: 42.4 us -> 0 us
  waiting for transfers between devices: 30.5 us -> 0 us
  starting transfers between devices: 22 us -> 0 us
  between operations: 14.3 us -> 0.67 us
  local copies, waits for them, and re-layouts: 14.7 us -> 4.66 us
  matrix products: 5.94 us -> 0 us
    all_to_all x4 -> x0, blocking collectives: 121 us -> none  [the longest x1 59.7 us: sum_at_owner(): lax.all_to_all(cut_along(array, dim, devices), axis, 0, 0, tiled=True)]
    pallas_call x0 -> x1, Pallas kernels: none -> 66.5 us  [local(): pl.pallas_call(kernel, out_shape=(jax.ShapeDtypeStruct((32, 128), F32), j...]
    another operation x4 -> x0, other arithmetic: 40.7 us -> none  [local(): lax.linalg.triangular_solve(whole_factor, whole_rest, left_side=True, low...]
    all_to_all x3 -> x0, waiting for transfers between devices: 30.4 us -> none  [the longest x1 15.3 us: sum_at_owner(): lax.all_to_all(cut_along(array, dim, devices), axis, 0, 0, tiled=True)]
    all_to_all x3 -> x0, starting transfers between devices: 22 us -> none  [the longest x2 18 us: copy_for_each(): lax.all_to_all(jnp.broadcast_to(array[None], (devices, *array.shape)), ax...]
    another operation x14 -> x0, local copies, waits for them, and re-layouts: 7.64 us -> none
    dot_general x2 -> x0, matrix products: 4.02 us -> none  [the longest x1 3.44 us: local(): lax.dot_general(band_rows, band_solution, (((0,), (0,)), ((), ())), preci...]
    unnamed x13, local copies, waits for them, and re-layouts: 1.85 us -> 4.66 us
  transfers between devices with their start and end apart: 4 -> 0, of which waited for: 2 -> 0; matrix products, arithmetic and copies ran while one was open for 21% -> 0% of each run, Pallas kernels for 0% -> 0%
where the time goes in v1:
time: 72.1 us; the launch traced here: 71.8 us
  Pallas kernels  66.5 us (92%)
  local copies, waits for them, and re-layouts  4.66 us (6%)
    pallas_call x1, Pallas kernels, local(): pl.pallas_call(kernel, out_shape=(jax.ShapeDtypeStruct((32, 128), F32), j...  66.5 us
    unnamed x13, local copies, waits for them, and re-layouts  4.66 us

profile of v1, /device:TPU:1, one launch (start us, length us, event | category | flops | bytes accessed | tf_op | source)
XLA Modules:
  0.0 71.8 jit_solution(14214012906757519905)
XLA Ops:
  0.6 0.0 copy-start.4
  0.6 0.0 copy-start.3
  0.6 0.8 %copy.8.lf = f32[32,16]{1,0:T(8,128)S(1)} copy(f32[32,16]{0,1:T(8,128)} %param.8) | data formatting | bytes 4096 | tf_op args[2]
  1.4 0.0 copy-done.4
  1.4 0.0 copy-done.3
  1.4 0.0 copy-start
  1.5 0.9 %copy-done = f32[256,256]{1,0:T(8,128)S(1)} copy-done((f32[256,256]{1,0:T(8,128)S(1)}, f32[256,256]{1,0:T(8,128)}, u32[]{:S(2)}) %copy-start) | copy-done | bytes 262168
  2.4 0.0 copy-start.1
  2.4 0.9 %copy-done.1 = f32[256,128]{1,0:T(8,128)S(1)} copy-done((f32[256,128]{1,0:T(8,128)S(1)}, f32[256,128]{1,0:T(8,128)}, u32[]{:S(2)}) %copy-start.1) | copy-done | bytes 131096
  3.3 0.0 copy-start.2
  3.3 0.8 %copy-done.2 = f32[32,256]{1,0:T(8,128)S(1)} copy-done((f32[32,256]{1,0:T(8,128)S(1)}, f32[32,256]{1,0:T(8,128)}, u32[]{:S(2)}) %copy-start.2) | copy-done | bytes 32792
  4.1 66.5 %shard_map.77 = (f32[32,128]{1,0:T(8,128)S(1)}, f32[256,128]{1,0:T(8,128)S(1)}) custom-call(f32[2,32]{1,0:T(2,128)S(1)} %copy-done.3, f32[2,128]{1,0:T(2,128)S(1)} %copy-done.4, f32[32,16]{1,0:T(8,128)S(1)} %copy.8.lf, f32[32,256]{1,0:T(8,128)S(1)} %copy-done.2, f32[256,256]{1,0:T(8,128)S(1)} %copy-done, f32[256,128]{1,0:T(8,128)S(1)} %copy-done.1), custom_call_target="tpu_custom_call" | custom-call | tf_op jit(solution)/shard_map/pallas_call | solution.py:385
  70.6 0.6 copy.11
  71.2 0.7 copy.12
Async XLA Ops:
  0.6 0.8 %copy-start.4 = (f32[2,128]{1,0:T(2,128)S(1)}, f32[2,128]{1,0:T(2,128)}, u32[]{:S(2)}) copy-start(f32[2,128]{1,0:T(2,128)} %ts.1) | copy-start | bytes 3076
  0.6 0.8 %copy-start.3 = (f32[2,32]{1,0:T(2,128)S(1)}, f32[2,32]{1,0:T(2,128)}, u32[]{:S(2)}) copy-start(f32[2,32]{1,0:T(2,128)} %bs.1) | copy-start | bytes 772
  1.4 1.0 %copy-start = (f32[256,256]{1,0:T(8,128)S(1)}, f32[256,256]{1,0:T(8,128)}, u32[]{:S(2)}) copy-start(f32[256,256]{1,0:T(8,128)} %s.1) | copy-start | bytes 786436
  2.4 0.9 %copy-start.1 = (f32[256,128]{1,0:T(8,128)S(1)}, f32[256,128]{1,0:T(8,128)}, u32[]{:S(2)}) copy-start(f32[256,128]{1,0:T(8,128)} %pc.1) | copy-start | bytes 393220
  3.3 0.8 %copy-start.2 = (f32[32,256]{1,0:T(8,128)S(1)}, f32[32,256]{1,0:T(8,128)}, u32[]{:S(2)}) copy-start(f32[32,256]{1,0:T(8,128)} %a.1) | copy-start | bytes 98308

commit v2 on v0

v2 whole, which is shorter than its diff:
```python
import jax
import jax.numpy as jnp
from jax import lax
from jax.experimental import pallas as pl
from jax.experimental.pallas import tpu as pltpu
from jax.sharding import PartitionSpec as P

length_scale = 0.3
MESH = pl.DeviceIdType.MESH
F32 = jnp.float32
BF16 = jnp.bfloat16
NZ, NY, NX = 8, 8, 4


def halves(value):
    high = value.astype(BF16)
    return high, (value - high.astype(F32)).astype(BF16)


def dot(a, b, dims):
    return lax.dot_general(a, b, (dims, ((), ())), preferred_element_type=F32)


def dot3(a, b, dims=((1,), (0,))):
    (ah, al), (bh, bl) = a, b
    return dot(ah, bh, dims) + (dot(ah, bl, dims) + dot(al, bh, dims))


def upper_inverses(blocks):
    n = 128
    i = lax.broadcasted_iota(jnp.int32, (n, n), 0)
    j = lax.broadcasted_iota(jnp.int32, (n, n), 1)
    done = []
    for u in blocks:
        inv = jnp.where(i == j, 1.0 / jnp.where(i == j, u, 1.0), 0.0)
        down = jnp.sum(inv, axis=1, keepdims=True)
        across = jnp.sum(inv, axis=0, keepdims=True)
        pair = (i // 2 == j // 2) & (i < j)
        done.append(inv - jnp.where(pair, u * down * across, 0.0))
    size = 2
    while size < n:
        part = (i // (2 * size) == j // (2 * size)) & (i // size < j // size)
        left = [halves(x) for x in done]
        mid = [dot3(x, halves(jnp.where(part, u, 0.0))) for x, u in zip(left, blocks)]
        done = [x - dot3(halves(m), xh) for x, m, xh in zip(done, mid, left)]
        size *= 2
    return done


def placed_at(value, offset):
    at = lax.broadcasted_iota(jnp.int32, (32, 128), 1)
    it = lax.broadcasted_iota(jnp.int32, (32, 128), 0)
    return lax.dot_general(
        value, (at == it + offset).astype(F32), (((1,), (0,)), ((), ())),
        precision=lax.Precision.HIGHEST, preferred_element_type=F32,
    )


NAMES = (
    "lz", "bz", "lp", "bp", "ly0", "ly1", "lx0", "lx1", "lq0", "lq1", "w",
    "a", "ap", "ts", "rx", "cy", "cp", "ux", "uy", "ry", "rz",
)
K = {name: k for k, name in enumerate(NAMES)}
LOADS = ("lf", "bs", "a", "ts", "s", "pc")
TAKING = ((2, 8), (4, 6))
BLOCKS = [(j, q) for j in range(4) for q in range(j, 4)]
NEAR_FIRST = (1, 7, 2, 6, 3, 5, 4)
FAR_FIRST = (4, 3, 5, 2, 6, 1, 7)


def order_of(zz):
    turn = 2 * (zz % 2) - 1
    return [(zz // 2 + o) % 4 for o in (0, 4 + turn, 4 - turn, 2)]


def kernel(
    bs_in, ts_in, lf_in, a_in, s_in, pc_in, v_out, cov_out,
    bs, ts, lf, a, s, pc,
    abuf, sh, sl, pb, xb, xs, ub, tsb, tsr, lps, lzo, lzp, lt16, lt, wf, wh, wl,
    cr, own, rr, zb, rc, vs,
    load, send, rec, a_rec, ap_rec, ux_rec, uy_rec, ry_rec, rz_rec,
):
    row = lax.axis_index("row")
    col = lax.axis_index("col")
    z, core = row // 2, row % 2
    y, x = col // NX, col % NX
    partner = (2 * z + 1 - core, col)
    takes = core == x // 2
    rests = core != x // 2
    half = x % 2
    order = order_of(z)

    def at_z(zz):
        return (2 * zz + core, col)

    def at_y(yy):
        return (row, yy * NX + x)

    def at_x(xx):
        return (row, y * NX + xx)

    def push(src, dst, name, device, recv=None):
        pltpu.make_async_remote_copy(
            src_ref=src,
            dst_ref=dst,
            send_sem=send.at[K[name]],
            recv_sem=rec.at[K[name]] if recv is None else recv,
            device_id=device,
            device_id_type=MESH,
        ).start()

    def await_bytes(ref, sem):
        pltpu.make_async_copy(ref, ref, sem).wait()

    with jax.named_scope("signals"):
        barrier = pltpu.get_barrier_semaphore()
        peers = []
        for d in FAR_FIRST:
            peers += [at_z((z + d) % NZ), at_y((y + d) % NY)]
        peers += [at_x((x + d) % NX) for d in (2, 1, 3)] + [partner]
        for peer in peers:
            pl.semaphore_signal(barrier, inc=1, device_id=peer, device_id_type=MESH)
    into = dict(lf=(lf_in, lf), bs=(bs_in, bs), a=(a_in, a), ts=(ts_in, ts), s=(s_in, s), pc=(pc_in, pc))
    loads = {n: pltpu.make_async_copy(*into[n], load.at[k]) for k, n in enumerate(LOADS)}
    for n in LOADS:
        loads[n].start()

    with jax.named_scope("prepare"):
        loads["lf"].wait()
        lps[0] = placed_at(lf[0:8], 32 * core) + placed_at(lf[8:16], 64 + 32 * core)
        loads["bs"].wait()
        lps[1] = jnp.zeros((8, 128), F32)
        lps[1, 0:2] = placed_at(bs[...], 32 * (row % 4))
        loads["a"].wait()

    with jax.named_scope("barrier"):
        pl.semaphore_wait(barrier, len(peers))

    root = takes & (y == z)
    with jax.named_scope("first_sends"):
        for d in FAR_FIRST:
            push(lps.at[0], lzo.at[0, z], "lz", at_z((z + d) % NZ))
        push(a, abuf.at[z, core], "ap", partner, ap_rec.at[z])
        for d in NEAR_FIRST:
            push(a, abuf.at[z, core], "a", at_z((z + d) % NZ), a_rec.at[z])
        for d in FAR_FIRST:
            push(lps.at[1], lzo.at[1, z], "bz", at_z((z + d) % NZ))
        abuf[z, core] = a[...]
        lzo[:, z] = lps[...]
        loads["ts"].wait()

        @pl.when(root)
        def _():
            for k in range(2):
                tsb[:, k] = jnp.broadcast_to(ts[k : k + 1], (128, 128)).T.reshape(NY, 16, 128)
            for d in FAR_FIRST:
                yy = (y + d) % NY
                push(tsb.at[yy], tsr, "ts", at_y(yy))
            tsr[...] = tsb[y]

        loads["s"].wait()
        sh[...], sl[...] = halves(s[...].T)

    def pass_on(o):
        with jax.named_scope("pass_on"):
            for zz in (2 * order[o], 2 * order[o] + 1):

                @pl.when(zz != z)
                def _():
                    await_bytes(a, a_rec.at[zz])
                    push(abuf.at[zz, core], abuf.at[zz, core], "ap", partner, ap_rec.at[zz])

    def product(o):
        p = order[o]
        with jax.named_scope("a_wait"):
            for zz in (2 * p, 2 * p + 1):
                await_bytes(a, ap_rec.at[zz])
        with jax.named_scope("product"):
            rows = abuf[pl.ds(2 * p, 2)].reshape(128, 256)
            out = dot3((sh[...], sl[...]), halves(rows), ((1,), (1,)))
            pb[o] = out.reshape(2, NY, 16, 128)
            for h in range(2):
                xx = 2 * core + h

                @pl.when(xx != x)
                def _():
                    push(pb.at[o, h], xb.at[o, x], "ux", at_x(xx), ux_rec.at[o])

                @pl.when(xx == x)
                def _():
                    xb[o, x] = pb[o, h]

    def x_sum(o):
        with jax.named_scope("x_wait"):
            await_bytes(xb.at[o, 0:3], ux_rec.at[o])
        with jax.named_scope("x_sum"):
            xs[o] = (xb[o, 0] + xb[o, 1]) + (xb[o, 2] + xb[o, 3])
            for d in FAR_FIRST:
                yy = (y + d) % NY
                push(xs.at[o, yy], ub.at[o, y], "uy", at_y(yy), uy_rec.at[o])
            ub[o, y] = xs[o, y]

    def cross():
        with jax.named_scope("cross"):

            @pl.when(y != z)
            def _():
                await_bytes(tsr, rec.at[K["ts"]])

            await_bytes(lzp.at[1], rec.at[K["bp"]])
            for p in range(4):
                spots = (lzo[1, 2 * p] + lzp[1, 2 * p]) + (lzo[1, 2 * p + 1] + lzp[1, 2 * p + 1])
                dx = tsr[0] - spots[0:1]
                dy = tsr[1] - spots[1:2]
                scaled = jnp.sqrt(dx * dx + dy * dy + 1e-06) * (3.0**0.5 / length_scale)
                cr[p] = (1.0 + scaled) * jnp.exp(-scaled)

    def y_sum(o):
        with jax.named_scope("y_wait"):
            await_bytes(ub.at[o, 0:7], uy_rec.at[o])
        with jax.named_scope("y_sum"):
            p = order[o]
            terms = [ub[o, k] for k in range(NY)]
            while len(terms) > 1:
                terms = [terms[i] + terms[i + 1] for i in range(0, len(terms), 2)]
            value = cr[p] - terms[0]
            own[o] = value
            for d in FAR_FIRST:
                push(own.at[o], zb.at[o, z], "rz", at_z((z + d) % NZ), rz_rec.at[o])
            for d in FAR_FIRST:
                push(own.at[o], rr.at[p, half, y], "ry", at_y((y + d) % NY), ry_rec.at[o])
            rr[p, half, y] = value
            zb[o, z] = value

    def forward(o):
        with jax.named_scope("z_wait"):
            await_bytes(zb.at[0, 0:7], rz_rec.at[o])
        with jax.named_scope("to_column"):
            for zz in range(NZ):
                p = order_of(zz)[o]

                @pl.when(zz != y)
                def _():
                    push(zb.at[o, zz], rc.at[p, y], "cy", at_y(zz))

                @pl.when(zz == y)
                def _():
                    rc[p, y] = zb[o, zz]

        with jax.named_scope("r_wait"):
            await_bytes(rr.at[0, 0, 0:7], ry_rec.at[o])
        with jax.named_scope("to_row"):
            for d in (2, 1, 3):
                there = rr.at[order[o], half]
                push(there, there, "rx", at_x((x + d) % NX))

    first_taking = 2 + 2 * core
    second_taking = 8 - 2 * core
    first_in = y < first_taking
    second_in = y < second_taking

    def await_some(slot, count, options, name):
        for n in options:

            @pl.when(count == n)
            def _():
                await_bytes(lt.at[0, slot, 0:n, 0], rec.at[K[name]])

    def factor_z():
        with jax.named_scope("factor_z"):
            await_bytes(lzo.at[0, 0:7], rec.at[K["lz"]])
            push(lzo.at[0], lzp.at[0], "lp", partner)

    def sites_z():
        with jax.named_scope("sites_z"):
            await_bytes(lzo.at[1, 0:7], rec.at[K["bz"]])
            push(lzo.at[1], lzp.at[1], "bp", partner)

    def factor_y():
        with jax.named_scope("factor_y"):
            await_bytes(lzp.at[0], rec.at[K["lp"]])
            low = lax.broadcasted_iota(jnp.int32, (8, 128), 1) < 64
            for q in range(4):
                t0, t1 = (lzo[0, k] + lzp[0, k] for k in (2 * q, 2 * q + 1))
                lt16[q, 0:8] = jnp.where(low, t0, pltpu.roll(t1, 64, 1))
                lt16[q, 8:16] = jnp.where(low, pltpu.roll(t0, 64, 1), t1)
            lt[core, 0, y, x] = lt16[core]
            lt[core, 1, y, x] = lt16[3 - core]

            def along_y(slot):
                here = lt.at[core, slot, y, x]
                for d in FAR_FIRST:
                    push(here, here, f"ly{slot}", at_y((y + d) % NY))

            pl.when(first_in)(lambda: along_y(0))
            pl.when(second_in)(lambda: along_y(1))

    def each_part(body):
        for k in range(2):

            @pl.when(core == k)
            def _():
                for slot in range(2):
                    body(k, slot, TAKING[k][slot])

    def factor_x():
        with jax.named_scope("factor_x"):
            await_some(0, first_taking - first_in.astype(jnp.int32), (1, 2, 3, 4), "ly0")
            await_some(1, second_taking - second_in.astype(jnp.int32), (5, 6, 7), "ly1")

            def along_x(k, slot, n):
                part = lt.at[k, slot, 0:n, x]
                for d in (2, 1, 3):
                    push(part, part, f"lx{slot}", at_x((x + d) % NX))

            each_part(along_x)

    def factor_arrives():
        with jax.named_scope("factor_arrives"):
            each_part(lambda k, slot, n: await_bytes(lt.at[k, slot, 0:n, 0:3], rec.at[K[f"lx{slot}"]]))

    def factor_pair():
        with jax.named_scope("factor_pair"):

            def across(k, slot, n):
                part = lt.at[k, slot, 0:n]
                push(part, part, f"lq{slot}", partner)

            each_part(across)

    def inverse():
        where = {0: (0, 0), 3: (0, 1), 1: (1, 0), 2: (1, 1)}

        def tile(j, q):
            k, slot = where[q]
            return lt[k, slot, 2 * j : 2 * j + 2].reshape(128, 128)

        def block(j, q):
            return halves(tile(j, q))

        with jax.named_scope("pair_wait"):
            for k in range(2):

                @pl.when(core == 1 - k)
                def _():
                    for slot in range(2):
                        await_bytes(lt.at[k, slot, 0 : TAKING[k][slot]], rec.at[K[f"lq{slot}"]])

        with jax.named_scope("inverse"):
            w = upper_inverses([tile(q, q) for q in range(4)])
            ws = [halves(v) for v in w]
            w01 = -dot3(halves(dot3(ws[0], block(0, 1))), ws[1])
            w23 = -dot3(halves(dot3(ws[2], block(2, 3))), ws[3])
            h01, h23 = halves(w01), halves(w23)
            t02 = halves(dot3(ws[0], block(0, 2)) + dot3(h01, block(1, 2)))
            t03 = halves(dot3(ws[0], block(0, 3)) + dot3(h01, block(1, 3)))
            t12 = halves(dot3(ws[1], block(1, 2)))
            t13 = halves(dot3(ws[1], block(1, 3)))
            w02 = -dot3(t02, ws[2])
            w03 = -(dot3(t02, h23) + dot3(t03, ws[3]))
            w12 = -dot3(t12, ws[2])
            w13 = -(dot3(t12, h23) + dot3(t13, ws[3]))
            full = {(0, 0): w[0], (1, 1): w[1], (2, 2): w[2], (3, 3): w[3]}
            full.update({(0, 1): w01, (2, 3): w23, (0, 2): w02, (0, 3): w03, (1, 2): w12, (1, 3): w13})
            for k, at in enumerate(BLOCKS):
                wf[k] = full[at]
            push(wf, wf, "w", partner)

    def split_inverse():
        with jax.named_scope("split"):
            for k, (j, q) in enumerate(BLOCKS):
                here = (slice(128 * j, 128 * j + 128), slice(128 * q, 128 * q + 128))
                wh[here], wl[here] = halves(wf[k])

    with jax.named_scope("zeros"):
        for j in range(1, 4):
            for ref in (wh, wl):
                ref[128 * j : 128 * j + 128, 0 : 128 * j] = jnp.zeros((128, 128 * j), BF16)

    pass_on(0)
    pass_on(1)
    product(0)
    factor_z()
    pass_on(2)
    product(1)
    factor_y()
    pass_on(3)
    product(2)
    sites_z()
    product(3)

    @pl.when(takes)
    def _():
        x_sum(0)
        x_sum(1)
        cross()
        x_sum(2)
        x_sum(3)
        factor_x()
        for o in range(4):
            y_sum(o)
        forward(0)
        factor_arrives()
        factor_pair()
        forward(1)
        forward(2)
        forward(3)
        with jax.named_scope("inverse_wait"):
            await_bytes(wf, rec.at[K["w"]])

    @pl.when(rests)
    def _():
        factor_x()
        factor_arrives()
        inverse()

    split_inverse()

    with jax.named_scope("column_wait"):

        @pl.when(takes)
        def _():
            await_bytes(rc.at[:, 0:7], rec.at[K["cy"]])
            push(rc, rc, "cp", partner)

    with jax.named_scope("row_wait"):

        @pl.when(takes)
        def _():
            await_bytes(rr.at[:, 0], rec.at[K["rx"]])

        @pl.when(rests)
        def _():
            await_bytes(rr, rec.at[K["rx"]])

    with jax.named_scope("row_solve"):
        solver = (wh[...], wl[...])
        right = jnp.concatenate([rr[p].reshape(256, 128) for p in range(4)], axis=1)
        vr = halves(dot3(halves(right), solver))
        loads["pc"].wait()
    with jax.named_scope("column_pair"):

        @pl.when(rests)
        def _():
            await_bytes(rc, rec.at[K["cp"]])
            await_bytes(lzp.at[1], rec.at[K["bp"]])

    with jax.named_scope("update"):
        right = jnp.concatenate([rc[p].reshape(128, 128) for p in range(4)], axis=1)
        vc = dot3(halves(right), solver)
        cov_out[...] = pc[...] - dot3(vr, halves(vc), ((1,), (1,)))
        for p in range(4):
            vs[p] = vc[:, 128 * p : 128 * p + 128]
        vs[4] = vs[row // 4].T
        v_out[...] = vs[4, pl.ds(pl.multiple_of(32 * (row % 4), 32), 32)]

    with jax.named_scope("drain"):
        await_bytes(lzo.at[0, 0:7], send.at[K["lz"]])
        await_bytes(lzo.at[1, 0:7], send.at[K["bz"]])
        await_bytes(lzo.at[0], send.at[K["lp"]])
        await_bytes(lzo.at[1], send.at[K["bp"]])
        pl.when(first_in)(lambda: await_bytes(lt.at[0, 0, 0:7, 0], send.at[K["ly0"]]))
        pl.when(second_in)(lambda: await_bytes(lt.at[0, 1, 0:7, 0], send.at[K["ly1"]]))
        each_part(lambda k, slot, n: await_bytes(lt.at[k, slot, 0:n, 0:3], send.at[K[f"lx{slot}"]]))
        await_bytes(abuf.at[0:7, 0], send.at[K["a"]])
        await_bytes(abuf.at[:, 0], send.at[K["ap"]])

        @pl.when(root)
        def _():
            await_bytes(tsb.at[0:7], send.at[K["ts"]])

        @pl.when(takes)
        def _():
            each_part(lambda k, slot, n: await_bytes(lt.at[k, slot, 0:n], send.at[K[f"lq{slot}"]]))
            await_bytes(xb.at[:, 0], send.at[K["ux"]])
            await_bytes(ub.at[:, 0:7], send.at[K["uy"]])
            await_bytes(zb.at[:, 0:7], send.at[K["rz"]])
            await_bytes(zb.at[:, 0:7], send.at[K["ry"]])
            await_bytes(xb.at[:, 0:3], send.at[K["rx"]])
            await_bytes(rc.at[:, 0:7], send.at[K["cy"]])
            await_bytes(rc, send.at[K["cp"]])

        @pl.when(rests)
        def _():
            await_bytes(xb.at[:, 0:2], send.at[K["ux"]])
            await_bytes(wf, send.at[K["w"]])


def local(band_sites, test_sites, band_factor, prior_factor, prior_solution, prior_covariance):
    vmem = pl.BlockSpec(memory_space=pltpu.VMEM)
    hbm = pl.BlockSpec(memory_space=pltpu.HBM)
    arrays = [
        (2, 32), (2, 128), (16, 32), (32, 256), (256, 256), (256, 128),
        (8, 2, 32, 256),
        BF16, BF16,
        (4, 2, NY, 16, 128),
        (4, NX, NY, 16, 128),
        (4, NY, 16, 128),
        (4, NY, 16, 128),
        (NY, 2, 16, 128),
        (2, 16, 128),
        (2, 8, 128),
        (2, 8, 8, 128), (2, 8, 8, 128),
        (4, 16, 128),
        (2, 2, 8, 4, 16, 128),
        (10, 128, 128),
        None, None,
        (4, 16, 128), (4, 16, 128),
        (4, 2, NY, 16, 128),
        (4, NZ, 16, 128),
        (4, NY, 16, 128),
        (5, 128, 128),
    ]
    scratch = []
    for shape in arrays:
        if shape is BF16:
            scratch.append(pltpu.VMEM((256, 256), BF16))
        elif shape is None:
            scratch.append(pltpu.VMEM((512, 512), BF16))
        else:
            scratch.append(pltpu.VMEM(shape, F32))
    counts = (len(LOADS), len(NAMES), len(NAMES), 8, 8, 4, 4, 4, 4)
    scratch += [pltpu.SemaphoreType.DMA((n,)) for n in counts]
    return pl.pallas_call(
        kernel,
        out_shape=(
            pltpu.VMEM((32, 128), F32),
            pltpu.VMEM((256, 128), F32),
        ),
        in_specs=[hbm] * 6,
        out_specs=(vmem, vmem),
        scratch_shapes=scratch,
        compiler_params=pltpu.CompilerParams(
            collective_id=0, has_side_effects=True, vmem_limit_bytes=60 * 1024 * 1024
        ),
    )(band_sites, test_sites, band_factor.T, prior_factor, prior_solution, prior_covariance)


def solution(mesh):
    placed = (
        P(None, "row"),
        P(None, "col"),
        P("row", "col"),
        P("row", "col"),
        P("col", "row"),
        P("row", "col"),
    )
    return jax.shard_map(
        local,
        mesh=mesh,
        in_specs=placed,
        out_specs=(P("row", "col"), P("row", "col")),
        check_vma=False,
    )
```

time: 251 us -> 50.9 us (0.20)
  blocking collectives: 121 us -> 0 us
  Pallas kernels: 0 us -> 48.9 us
  other arithmetic: 42.4 us -> 0 us
  waiting for transfers between devices: 30.5 us -> 0 us
  starting transfers between devices: 22 us -> 0 us
  between operations: 14.3 us -> 0.64 us
  local copies, waits for them, and re-layouts: 14.7 us -> 1.26 us
  matrix products: 5.94 us -> 0 us
    all_to_all x4 -> x0, blocking collectives: 121 us -> none  [the longest x1 59.7 us: sum_at_owner(): lax.all_to_all(cut_along(array, dim, devices), axis, 0, 0, tiled=True)]
    pallas_call x0 -> x1, Pallas kernels: none -> 48.9 us  [local(): pl.pallas_call(kernel, out_shape=(pltpu.VMEM((32, 128), F32), pltpu.VMEM(...]
    another operation x4 -> x0, other arithmetic: 40.7 us -> none  [local(): lax.linalg.triangular_solve(whole_factor, whole_rest, left_side=True, low...]
    all_to_all x3 -> x0, waiting for transfers between devices: 30.4 us -> none  [the longest x1 15.3 us: sum_at_owner(): lax.all_to_all(cut_along(array, dim, devices), axis, 0, 0, tiled=True)]
    all_to_all x3 -> x0, starting transfers between devices: 22 us -> none  [the longest x2 18 us: copy_for_each(): lax.all_to_all(jnp.broadcast_to(array[None], (devices, *array.shape)), ax...]
    another operation x14 -> x0, local copies, waits for them, and re-layouts: 7.64 us -> none
    dot_general x2 -> x0, matrix products: 4.02 us -> none  [the longest x1 3.44 us: local(): lax.dot_general(band_rows, band_solution, (((0,), (0,)), ((), ())), preci...]
  transfers between devices with their start and end apart: 4 -> 0, of which waited for: 2 -> 0; matrix products, arithmetic and copies ran while one was open for 21% -> 0% of each run, Pallas kernels for 0% -> 0%
where the time goes in v2:
time: 50.9 us; the launch traced here: 50.8 us
  Pallas kernels  48.9 us (96%)
  local copies, waits for them, and re-layouts  1.26 us (2%)
  between operations  0.64 us (1%)
    pallas_call x1, Pallas kernels, local(): pl.pallas_call(kernel, out_shape=(pltpu.VMEM((32, 128), F32), pltpu.VMEM(...  48.9 us
    unnamed x2, local copies, waits for them, and re-layouts  1.26 us

profile of v2, /device:TPU:1, one launch (start us, length us, event | category | flops | bytes accessed | tf_op | source)
XLA Modules:
  0.0 50.8 jit_solution(17973037294324182480)
XLA Ops:
  0.6 48.9 %shard_map.77 = (f32[32,128]{1,0:T(8,128)S(1)}, f32[256,128]{1,0:T(8,128)S(1)}) custom-call(f32[2,32]{1,0:T(2,128)} %bs_in.1, f32[2,128]{1,0:T(2,128)} %ts_in.1, f32[16,32]{1,0:T(8,128)} %bitcast.1, f32[32,256]{1,0:T(8,128)} %a_in.1, f32[256,256]{1,0:T(8,128)} %s_in.1, f32[256,128]{1,0:T(8,128)} %pc_in.1), custom_call_target="tpu_custom_call" | custom-call | tf_op jit(solution)/shard_map/pallas_call | solution.py:524
  49.5 0.6 %copy.10 = f32[32,128]{1,0:T(8,128)} copy(f32[32,128]{1,0:T(8,128)S(1)} %get-tuple-element.2) | data formatting | bytes 32768
  50.1 0.7 %copy.11 = f32[256,128]{1,0:T(8,128)} copy(f32[256,128]{1,0:T(8,128)S(1)} %get-tuple-element.3) | data formatting | bytes 262144

commit v3 on v2

--- a/solution.py
+++ b/solution.py
@@ -58,7 +58,7 @@
 
 NAMES = (
     "lz", "bz", "lp", "bp", "ly0", "ly1", "lx0", "lx1", "lq0", "lq1", "w",
-    "a", "ap", "ts", "rx", "cy", "cp", "ux", "uy", "ry", "rz",
+    "a", "ap", "ts", "rx", "cy", "ux", "uy", "ry", "rz", "cp", "hy", "hx", "hg", "hf", "cd",
 )
 K = {name: k for k, name in enumerate(NAMES)}
 LOADS = ("lf", "bs", "a", "ts", "s", "pc")
@@ -68,6 +68,15 @@
 FAR_FIRST = (4, 3, 5, 2, 6, 1, 7)
 
 
+LAST = 3
+
+
+def added(terms):
+    while len(terms) > 1:
+        terms = [terms[i] + terms[i + 1] for i in range(0, len(terms), 2)]
+    return terms[0]
+
+
 def order_of(zz):
     turn = 2 * (zz % 2) - 1
     return [(zz // 2 + o) % 4 for o in (0, 4 + turn, 4 - turn, 2)]
@@ -76,9 +85,9 @@
 def kernel(
     bs_in, ts_in, lf_in, a_in, s_in, pc_in, v_out, cov_out,
     bs, ts, lf, a, s, pc,
-    abuf, sh, sl, pb, xb, xs, ub, tsb, tsr, lps, lzo, lzp, lt16, lt, wf, wh, wl,
-    cr, own, rr, zb, rc, vs,
-    load, send, rec, a_rec, ap_rec, ux_rec, uy_rec, ry_rec, rz_rec,
+    abuf, sh, sl, pb, xb, xs, ub, hb, hs, hx, hg, tsb, tsr, lps, bss, lzo, lzp, bzo, bzp, lt16, lt, wf, wh, wl,
+    cr, own, rr, zb, rc, acc, vs,
+    load, send, rec, a_rec, ap_rec, ux_rec, uy_rec, ry_rec, rz_rec, rx_rec, cy_rec, cp_rec, hy_rec, hx_rec, hg_rec, hf_rec,
 ):
     row = lax.axis_index("row")
     col = lax.axis_index("col")
@@ -88,10 +97,15 @@
     takes = core == x // 2
     rests = core != x // 2
     half = x % 2
+    next_x = 2 * core + 1 - half
+    far_x = (x + 2) % NX
     order = order_of(z)
 
     def at_z(zz):
         return (2 * zz + core, col)
+
+    def across_z(zz):
+        return (2 * zz + 1 - core, col)
 
     def at_y(yy):
         return (row, yy * NX + x)
@@ -120,6 +134,12 @@
         peers += [at_x((x + d) % NX) for d in (2, 1, 3)] + [partner]
         for peer in peers:
             pl.semaphore_signal(barrier, inc=1, device_id=peer, device_id_type=MESH)
+
+        @pl.when(rests)
+        def _():
+            for d in FAR_FIRST:
+                pl.semaphore_signal(barrier, inc=1, device_id=across_z((z + d) % NZ), device_id_type=MESH)
+
     into = dict(lf=(lf_in, lf), bs=(bs_in, bs), a=(a_in, a), ts=(ts_in, ts), s=(s_in, s), pc=(pc_in, pc))
     loads = {n: pltpu.make_async_copy(*into[n], load.at[k]) for k, n in enumerate(LOADS)}
     for n in LOADS:
@@ -127,26 +147,27 @@
 
     with jax.named_scope("prepare"):
         loads["lf"].wait()
-        lps[0] = placed_at(lf[0:8], 32 * core) + placed_at(lf[8:16], 64 + 32 * core)
+        lps[...] = placed_at(lf[0:8], 32 * core) + placed_at(lf[8:16], 64 + 32 * core)
         loads["bs"].wait()
-        lps[1] = jnp.zeros((8, 128), F32)
-        lps[1, 0:2] = placed_at(bs[...], 32 * (row % 4))
+        bss[...] = placed_at(bs[...], 32 * (row % 4))
         loads["a"].wait()
 
     with jax.named_scope("barrier"):
-        pl.semaphore_wait(barrier, len(peers))
+        pl.when(takes)(lambda: pl.semaphore_wait(barrier, len(peers) + NZ - 1))
+        pl.when(rests)(lambda: pl.semaphore_wait(barrier, len(peers)))
 
     root = takes & (y == z)
     with jax.named_scope("first_sends"):
         for d in FAR_FIRST:
-            push(lps.at[0], lzo.at[0, z], "lz", at_z((z + d) % NZ))
+            push(lps, lzo.at[z], "lz", at_z((z + d) % NZ))
         push(a, abuf.at[z, core], "ap", partner, ap_rec.at[z])
         for d in NEAR_FIRST:
             push(a, abuf.at[z, core], "a", at_z((z + d) % NZ), a_rec.at[z])
         for d in FAR_FIRST:
-            push(lps.at[1], lzo.at[1, z], "bz", at_z((z + d) % NZ))
+            push(bss, bzo.at[z], "bz", at_z((z + d) % NZ))
         abuf[z, core] = a[...]
-        lzo[:, z] = lps[...]
+        lzo[z] = lps[...]
+        bzo[z] = bss[...]
         loads["ts"].wait()
 
         @pl.when(root)
@@ -179,22 +200,36 @@
             rows = abuf[pl.ds(2 * p, 2)].reshape(128, 256)
             out = dot3((sh[...], sl[...]), halves(rows), ((1,), (1,)))
             pb[o] = out.reshape(2, NY, 16, 128)
-            for h in range(2):
-                xx = 2 * core + h
-
-                @pl.when(xx != x)
-                def _():
-                    push(pb.at[o, h], xb.at[o, x], "ux", at_x(xx), ux_rec.at[o])
-
-                @pl.when(xx == x)
-                def _():
-                    xb[o, x] = pb[o, h]
+            push(pb.at[o, 1 - half], xb.at[o, rests.astype(jnp.int32)], "ux", at_x(next_x), ux_rec.at[o])
+
+            @pl.when(rests)
+            def _():
+                for d in FAR_FIRST:
+                    yy = (y + d) % NY
+                    push(pb.at[o, half, yy], hb.at[o, y], "hy", at_y(yy), hy_rec.at[o])
+                hb[o, y] = pb[o, half, y]
+
+    def helper_sum(o):
+        with jax.named_scope("helper_wait"):
+            await_bytes(hb.at[o, 0:7], hy_rec.at[o])
+        with jax.named_scope("helper_sum"):
+            hs[o] = added([hb[o, k] for k in range(NY)])
+            push(hs.at[o], hx.at[o], "hx", at_x(far_x), hx_rec.at[o])
+
+    def helper_forward(o):
+        with jax.named_scope("helper_wait"):
+            await_bytes(hg.at[o], hg_rec.at[o])
+        with jax.named_scope("helper_forward"):
+            p = order[o]
+            for d in FAR_FIRST:
+                push(hg.at[o], rr.at[p, half, y], "hf", at_y((y + d) % NY), hf_rec.at[o])
+            rr[p, half, y] = hg[o]
 
     def x_sum(o):
         with jax.named_scope("x_wait"):
-            await_bytes(xb.at[o, 0:3], ux_rec.at[o])
+            await_bytes(xb.at[o], ux_rec.at[o])
         with jax.named_scope("x_sum"):
-            xs[o] = (xb[o, 0] + xb[o, 1]) + (xb[o, 2] + xb[o, 3])
+            xs[o] = (xb[o, 0] + xb[o, 1]) + pb[o, half]
             for d in FAR_FIRST:
                 yy = (y + d) % NY
                 push(xs.at[o, yy], ub.at[o, y], "uy", at_y(yy), uy_rec.at[o])
@@ -207,9 +242,9 @@
             def _():
                 await_bytes(tsr, rec.at[K["ts"]])
 
-            await_bytes(lzp.at[1], rec.at[K["bp"]])
+            await_bytes(bzp, rec.at[K["bp"]])
             for p in range(4):
-                spots = (lzo[1, 2 * p] + lzp[1, 2 * p]) + (lzo[1, 2 * p + 1] + lzp[1, 2 * p + 1])
+                spots = (bzo[2 * p] + bzp[2 * p]) + (bzo[2 * p + 1] + bzp[2 * p + 1])
                 dx = tsr[0] - spots[0:1]
                 dy = tsr[1] - spots[1:2]
                 scaled = jnp.sqrt(dx * dx + dy * dy + 1e-06) * (3.0**0.5 / length_scale)
@@ -218,41 +253,55 @@
     def y_sum(o):
         with jax.named_scope("y_wait"):
             await_bytes(ub.at[o, 0:7], uy_rec.at[o])
+            await_bytes(hx.at[o], hx_rec.at[o])
         with jax.named_scope("y_sum"):
             p = order[o]
-            terms = [ub[o, k] for k in range(NY)]
-            while len(terms) > 1:
-                terms = [terms[i] + terms[i + 1] for i in range(0, len(terms), 2)]
-            value = cr[p] - terms[0]
+            value = cr[p] - (added([ub[o, k] for k in range(NY)]) + hx[o])
             own[o] = value
+            push(own.at[o], hg.at[o], "hg", at_x(far_x), hg_rec.at[o])
             for d in FAR_FIRST:
                 push(own.at[o], zb.at[o, z], "rz", at_z((z + d) % NZ), rz_rec.at[o])
+                if o == LAST:
+                    push(own.at[o], zb.at[o, z], "cd", across_z((z + d) % NZ), rz_rec.at[o])
+            if o == LAST:
+                push(own.at[o], zb.at[o, z], "cd", partner, rz_rec.at[o])
             for d in FAR_FIRST:
                 push(own.at[o], rr.at[p, half, y], "ry", at_y((y + d) % NY), ry_rec.at[o])
             rr[p, half, y] = value
             zb[o, z] = value
 
-    def forward(o):
+    def to_column(o):
         with jax.named_scope("z_wait"):
-            await_bytes(zb.at[0, 0:7], rz_rec.at[o])
+            if o == LAST:
+                pl.when(takes)(lambda: await_bytes(zb.at[0, 0:7], rz_rec.at[o]))
+                pl.when(rests)(lambda: await_bytes(zb.at[0], rz_rec.at[o]))
+            else:
+                await_bytes(zb.at[0, 0:7], rz_rec.at[o])
         with jax.named_scope("to_column"):
             for zz in range(NZ):
                 p = order_of(zz)[o]
 
                 @pl.when(zz != y)
                 def _():
-                    push(zb.at[o, zz], rc.at[p, y], "cy", at_y(zz))
+                    push(zb.at[o, zz], rc.at[p, y], "cy", at_y(zz), cy_rec.at[o])
 
                 @pl.when(zz == y)
                 def _():
                     rc[p, y] = zb[o, zz]
 
+    def hand_over(o):
+        with jax.named_scope("hand_over"):
+            await_bytes(rc.at[0, 0:7], cy_rec.at[o])
+            there = rc.at[order_of(y)[o]]
+            push(there, there, "cp", partner, cp_rec.at[o])
+
+    def to_row(o):
         with jax.named_scope("r_wait"):
             await_bytes(rr.at[0, 0, 0:7], ry_rec.at[o])
         with jax.named_scope("to_row"):
-            for d in (2, 1, 3):
+            for d in (1, 3):
                 there = rr.at[order[o], half]
-                push(there, there, "rx", at_x((x + d) % NX))
+                push(there, there, "rx", at_x((x + d) % NX), rx_rec.at[o])
 
     first_taking = 2 + 2 * core
     second_taking = 8 - 2 * core
@@ -268,20 +317,20 @@
 
     def factor_z():
         with jax.named_scope("factor_z"):
-            await_bytes(lzo.at[0, 0:7], rec.at[K["lz"]])
-            push(lzo.at[0], lzp.at[0], "lp", partner)
+            await_bytes(lzo.at[0:7], rec.at[K["lz"]])
+            push(lzo, lzp, "lp", partner)
 
     def sites_z():
         with jax.named_scope("sites_z"):
-            await_bytes(lzo.at[1, 0:7], rec.at[K["bz"]])
-            push(lzo.at[1], lzp.at[1], "bp", partner)
+            await_bytes(bzo.at[0:7], rec.at[K["bz"]])
+            push(bzo, bzp, "bp", partner)
 
     def factor_y():
         with jax.named_scope("factor_y"):
-            await_bytes(lzp.at[0], rec.at[K["lp"]])
+            await_bytes(lzp, rec.at[K["lp"]])
             low = lax.broadcasted_iota(jnp.int32, (8, 128), 1) < 64
             for q in range(4):
-                t0, t1 = (lzo[0, k] + lzp[0, k] for k in (2 * q, 2 * q + 1))
+                t0, t1 = (lzo[k] + lzp[k] for k in (2 * q, 2 * q + 1))
                 lt16[q, 0:8] = jnp.where(low, t0, pltpu.roll(t1, 64, 1))
                 lt16[q, 8:16] = jnp.where(low, pltpu.roll(t0, 64, 1), t1)
             lt[core, 0, y, x] = lt16[core]
@@ -328,7 +377,7 @@
 
             each_part(across)
 
-    def inverse():
+    def inverse(between):
         where = {0: (0, 0), 3: (0, 1), 1: (1, 0), 2: (1, 1)}
 
         def tile(j, q):
@@ -346,8 +395,10 @@
                     for slot in range(2):
                         await_bytes(lt.at[k, slot, 0 : TAKING[k][slot]], rec.at[K[f"lq{slot}"]])
 
+        with jax.named_scope("diagonal"):
+            w = upper_inverses([tile(q, q) for q in range(4)])
+        between()
         with jax.named_scope("inverse"):
-            w = upper_inverses([tile(q, q) for q in range(4)])
             ws = [halves(v) for v in w]
             w01 = -dot3(halves(dot3(ws[0], block(0, 1))), ws[1])
             w23 = -dot3(halves(dot3(ws[2], block(2, 3))), ws[3])
@@ -378,12 +429,12 @@
                 ref[128 * j : 128 * j + 128, 0 : 128 * j] = jnp.zeros((128, 128 * j), BF16)
 
     pass_on(0)
+    factor_z()
     pass_on(1)
     product(0)
-    factor_z()
+    factor_y()
     pass_on(2)
     product(1)
-    factor_y()
     pass_on(3)
     product(2)
     sites_z()
@@ -395,59 +446,76 @@
         x_sum(1)
         cross()
         x_sum(2)
+        factor_x()
         x_sum(3)
-        factor_x()
-        for o in range(4):
-            y_sum(o)
-        forward(0)
+        y_sum(0)
+        y_sum(1)
         factor_arrives()
         factor_pair()
-        forward(1)
-        forward(2)
-        forward(3)
+        y_sum(2)
+        y_sum(3)
+        for o in range(4):
+            to_column(o)
+            to_row(o)
+        hand_over(0)
         with jax.named_scope("inverse_wait"):
             await_bytes(wf, rec.at[K["w"]])
+        hand_over(1)
+
+    def first_two():
+        helper_forward(0)
+        helper_forward(1)
 
     @pl.when(rests)
     def _():
+        helper_sum(0)
+        helper_sum(1)
         factor_x()
+        helper_sum(2)
+        helper_sum(3)
         factor_arrives()
-        inverse()
+        inverse(first_two)
+        helper_forward(2)
+        helper_forward(3)
+        to_column(LAST)
+        await_bytes(bzp, rec.at[K["bp"]])
 
     split_inverse()
 
-    with jax.named_scope("column_wait"):
-
-        @pl.when(takes)
-        def _():
-            await_bytes(rc.at[:, 0:7], rec.at[K["cy"]])
-            push(rc, rc, "cp", partner)
-
-    with jax.named_scope("row_wait"):
-
-        @pl.when(takes)
-        def _():
-            await_bytes(rr.at[:, 0], rec.at[K["rx"]])
-
-        @pl.when(rests)
-        def _():
-            await_bytes(rr, rec.at[K["rx"]])
-
-    with jax.named_scope("row_solve"):
-        solver = (wh[...], wl[...])
-        right = jnp.concatenate([rr[p].reshape(256, 128) for p in range(4)], axis=1)
-        vr = halves(dot3(halves(right), solver))
-        loads["pc"].wait()
-    with jax.named_scope("column_pair"):
-
-        @pl.when(rests)
-        def _():
-            await_bytes(rc, rec.at[K["cp"]])
-            await_bytes(lzp.at[1], rec.at[K["bp"]])
-
+    def solved(chunks, rights):
+        rows = [pl.ds(pl.multiple_of(128 * p, 128), 128) for p in chunks]
+        solver = [jnp.concatenate([ref[at] for at in rows], axis=0) for ref in (wh, wl)]
+        return dot3(halves(jnp.concatenate(rights, axis=1)), solver)
+
+    def row_part(turns):
+        with jax.named_scope("row_wait"):
+            for o in turns:
+                await_bytes(rr.at[0, 0], rx_rec.at[o])
+                pl.when(rests)(lambda: await_bytes(rr.at[0, 0, 0:7], hf_rec.at[o]))
+        with jax.named_scope("row_solve"):
+            chunks = [order[o] for o in turns]
+            return solved(chunks, [rr[p].reshape(256, 128) for p in chunks])
+
+    def column_part(turns):
+        with jax.named_scope("column_wait"):
+
+            for o in turns:
+                if o == LAST:
+                    await_bytes(rc.at[0, 0:7], cy_rec.at[o])
+                else:
+                    pl.when(rests)(lambda: await_bytes(rc.at[0], cp_rec.at[o]))
+
+        with jax.named_scope("column_solve"):
+            chunks = [order_of(y)[o] for o in turns]
+            return solved(chunks, [rc[p].reshape(128, 128) for p in chunks])
+
+    acc[0:256] = row_part((0, 1, 2))
+    pl.when(takes)(lambda: hand_over(2))
+    acc[256:384] = column_part((0, 1, 2))
+    vr = halves(acc[0:256] + row_part((3,)))
+    loads["pc"].wait()
+    vc = acc[256:384] + column_part((3,))
     with jax.named_scope("update"):
-        right = jnp.concatenate([rc[p].reshape(128, 128) for p in range(4)], axis=1)
-        vc = dot3(halves(right), solver)
         cov_out[...] = pc[...] - dot3(vr, halves(vc), ((1,), (1,)))
         for p in range(4):
             vs[p] = vc[:, 128 * p : 128 * p + 128]
@@ -455,15 +523,16 @@
         v_out[...] = vs[4, pl.ds(pl.multiple_of(32 * (row % 4), 32), 32)]
 
     with jax.named_scope("drain"):
-        await_bytes(lzo.at[0, 0:7], send.at[K["lz"]])
-        await_bytes(lzo.at[1, 0:7], send.at[K["bz"]])
-        await_bytes(lzo.at[0], send.at[K["lp"]])
-        await_bytes(lzo.at[1], send.at[K["bp"]])
+        await_bytes(lzo.at[0:7], send.at[K["lz"]])
+        await_bytes(bzo.at[0:7], send.at[K["bz"]])
+        await_bytes(lzo, send.at[K["lp"]])
+        await_bytes(bzo, send.at[K["bp"]])
         pl.when(first_in)(lambda: await_bytes(lt.at[0, 0, 0:7, 0], send.at[K["ly0"]]))
         pl.when(second_in)(lambda: await_bytes(lt.at[0, 1, 0:7, 0], send.at[K["ly1"]]))
         each_part(lambda k, slot, n: await_bytes(lt.at[k, slot, 0:n, 0:3], send.at[K[f"lx{slot}"]]))
         await_bytes(abuf.at[0:7, 0], send.at[K["a"]])
         await_bytes(abuf.at[:, 0], send.at[K["ap"]])
+        await_bytes(xb.at[:, 0], send.at[K["ux"]])
 
         @pl.when(root)
         def _():
@@ -472,17 +541,21 @@
         @pl.when(takes)
         def _():
             each_part(lambda k, slot, n: await_bytes(lt.at[k, slot, 0:n], send.at[K[f"lq{slot}"]]))
-            await_bytes(xb.at[:, 0], send.at[K["ux"]])
+            await_bytes(own, send.at[K["hg"]])
             await_bytes(ub.at[:, 0:7], send.at[K["uy"]])
             await_bytes(zb.at[:, 0:7], send.at[K["rz"]])
+            await_bytes(rc.at[:, 0:7], send.at[K["cy"]])
+            await_bytes(rc.at[0:3], send.at[K["cp"]])
+            await_bytes(zb.at[0], send.at[K["cd"]])
             await_bytes(zb.at[:, 0:7], send.at[K["ry"]])
-            await_bytes(xb.at[:, 0:3], send.at[K["rx"]])
-            await_bytes(rc.at[:, 0:7], send.at[K["cy"]])
-            await_bytes(rc, send.at[K["cp"]])
+            await_bytes(xb, send.at[K["rx"]])
 
         @pl.when(rests)
         def _():
-            await_bytes(xb.at[:, 0:2], send.at[K["ux"]])
+            await_bytes(hb.at[:, 0:7], send.at[K["hy"]])
+            await_bytes(hs, send.at[K["hx"]])
+            await_bytes(rc.at[0, 0:7], send.at[K["cy"]])
+            await_bytes(hb.at[:, 0:7], send.at[K["hf"]])
             await_bytes(wf, send.at[K["w"]])
 
 
@@ -494,13 +567,16 @@
         (8, 2, 32, 256),
         BF16, BF16,
         (4, 2, NY, 16, 128),
-        (4, NX, NY, 16, 128),
+        (4, 2, NY, 16, 128),
         (4, NY, 16, 128),
         (4, NY, 16, 128),
+        (4, NY, 16, 128),
+        (4, 16, 128), (4, 16, 128), (4, 16, 128),
         (NY, 2, 16, 128),
         (2, 16, 128),
-        (2, 8, 128),
-        (2, 8, 8, 128), (2, 8, 8, 128),
+        (8, 128), (2, 128),
+        (8, 8, 128), (8, 8, 128),
+        (8, 2, 128), (8, 2, 128),
         (4, 16, 128),
         (2, 2, 8, 4, 16, 128),
         (10, 128, 128),
@@ -509,6 +585,7 @@
         (4, 2, NY, 16, 128),
         (4, NZ, 16, 128),
         (4, NY, 16, 128),
+        (384, 512),
         (5, 128, 128),
     ]
     scratch = []
@@ -519,7 +596,7 @@
             scratch.append(pltpu.VMEM((512, 512), BF16))
         else:
             scratch.append(pltpu.VMEM(shape, F32))
-    counts = (len(LOADS), len(NAMES), len(NAMES), 8, 8, 4, 4, 4, 4)
+    counts = (len(LOADS), len(NAMES), len(NAMES), 8, 8, *[4] * 11)
     scratch += [pltpu.SemaphoreType.DMA((n,)) for n in counts]
     return pl.pallas_call(
         kernel,

time: 50.9 us -> 52.3 us (1.028)
  Pallas kernels: 48.9 us -> 50.2 us
    pallas_call x1, Pallas kernels: 48.9 us -> 50.2 us  [local(): pl.pallas_call(kernel, out_shape=(pltpu.VMEM((32, 128), F32), pltpu.VMEM(...]
where the time goes in v3:
time: 52.3 us; the launch traced here: 52.1 us
  Pallas kernels  50.2 us (96%)
  local copies, waits for them, and re-layouts  1.26 us (2%)
  between operations  0.64 us (1%)
    pallas_call x1, Pallas kernels, local(): pl.pallas_call(kernel, out_shape=(pltpu.VMEM((32, 128), F32), pltpu.VMEM(...  50.2 us
    unnamed x2, local copies, waits for them, and re-layouts  1.26 us

profile of v3, /device:TPU:1, one launch (start us, length us, event | category | flops | bytes accessed | tf_op | source)
XLA Modules:
  0.0 52.1 jit_solution(3855665526770462039)
XLA Ops:
  0.6 50.2 %shard_map.77 = (f32[32,128]{1,0:T(8,128)S(1)}, f32[256,128]{1,0:T(8,128)S(1)}) custom-call(f32[2,32]{1,0:T(2,128)} %bs_in.1, f32[2,128]{1,0:T(2,128)} %ts_in.1, f32[16,32]{1,0:T(8,128)} %bitcast.1, f32[32,256]{1,0:T(8,128)} %a_in.1, f32[256,256]{1,0:T(8,128)} %s_in.1, f32[256,128]{1,0:T(8,128)} %pc_in.1), custom_call_target="tpu_custom_call" | custom-call | tf_op jit(solution)/shard_map/pallas_call | solution.py:601
  50.9 0.6 %copy.10 = f32[32,128]{1,0:T(8,128)} copy(f32[32,128]{1,0:T(8,128)S(1)} %get-tuple-element.2) | data formatting | bytes 32768
  51.5 0.7 %copy.11 = f32[256,128]{1,0:T(8,128)} copy(f32[256,128]{1,0:T(8,128)S(1)} %get-tuple-element.3) | data formatting | bytes 262144

commit v4 on v2

--- a/solution.py
+++ b/solution.py
@@ -58,7 +58,7 @@
 
 NAMES = (
     "lz", "bz", "lp", "bp", "ly0", "ly1", "lx0", "lx1", "lq0", "lq1", "w",
-    "a", "ap", "ts", "rx", "cy", "cp", "ux", "uy", "ry", "rz",
+    "a", "ap", "ts", "rx", "cy", "ux", "uy", "ry", "rz", "cp",
 )
 K = {name: k for k, name in enumerate(NAMES)}
 LOADS = ("lf", "bs", "a", "ts", "s", "pc")
@@ -76,9 +76,9 @@
 def kernel(
     bs_in, ts_in, lf_in, a_in, s_in, pc_in, v_out, cov_out,
     bs, ts, lf, a, s, pc,
-    abuf, sh, sl, pb, xb, xs, ub, tsb, tsr, lps, lzo, lzp, lt16, lt, wf, wh, wl,
-    cr, own, rr, zb, rc, vs,
-    load, send, rec, a_rec, ap_rec, ux_rec, uy_rec, ry_rec, rz_rec,
+    abuf, sh, sl, pb, xb, xs, ub, tsb, tsr, lps, bss, lzo, lzp, bzo, bzp, lt16, lt, wf, wh, wl,
+    cr, own, rr, zb, rc, acc, vs,
+    load, send, rec, a_rec, ap_rec, ux_rec, uy_rec, ry_rec, rz_rec, rx_rec, cy_rec, cp_rec,
 ):
     row = lax.axis_index("row")
     col = lax.axis_index("col")
@@ -120,6 +120,7 @@
         peers += [at_x((x + d) % NX) for d in (2, 1, 3)] + [partner]
         for peer in peers:
             pl.semaphore_signal(barrier, inc=1, device_id=peer, device_id_type=MESH)
+
     into = dict(lf=(lf_in, lf), bs=(bs_in, bs), a=(a_in, a), ts=(ts_in, ts), s=(s_in, s), pc=(pc_in, pc))
     loads = {n: pltpu.make_async_copy(*into[n], load.at[k]) for k, n in enumerate(LOADS)}
     for n in LOADS:
@@ -127,10 +128,9 @@
 
     with jax.named_scope("prepare"):
         loads["lf"].wait()
-        lps[0] = placed_at(lf[0:8], 32 * core) + placed_at(lf[8:16], 64 + 32 * core)
+        lps[...] = placed_at(lf[0:8], 32 * core) + placed_at(lf[8:16], 64 + 32 * core)
         loads["bs"].wait()
-        lps[1] = jnp.zeros((8, 128), F32)
-        lps[1, 0:2] = placed_at(bs[...], 32 * (row % 4))
+        bss[...] = placed_at(bs[...], 32 * (row % 4))
         loads["a"].wait()
 
     with jax.named_scope("barrier"):
@@ -139,14 +139,15 @@
     root = takes & (y == z)
     with jax.named_scope("first_sends"):
         for d in FAR_FIRST:
-            push(lps.at[0], lzo.at[0, z], "lz", at_z((z + d) % NZ))
+            push(lps, lzo.at[z], "lz", at_z((z + d) % NZ))
         push(a, abuf.at[z, core], "ap", partner, ap_rec.at[z])
         for d in NEAR_FIRST:
             push(a, abuf.at[z, core], "a", at_z((z + d) % NZ), a_rec.at[z])
         for d in FAR_FIRST:
-            push(lps.at[1], lzo.at[1, z], "bz", at_z((z + d) % NZ))
+            push(bss, bzo.at[z], "bz", at_z((z + d) % NZ))
         abuf[z, core] = a[...]
-        lzo[:, z] = lps[...]
+        lzo[z] = lps[...]
+        bzo[z] = bss[...]
         loads["ts"].wait()
 
         @pl.when(root)
@@ -207,9 +208,9 @@
             def _():
                 await_bytes(tsr, rec.at[K["ts"]])
 
-            await_bytes(lzp.at[1], rec.at[K["bp"]])
+            await_bytes(bzp, rec.at[K["bp"]])
             for p in range(4):
-                spots = (lzo[1, 2 * p] + lzp[1, 2 * p]) + (lzo[1, 2 * p + 1] + lzp[1, 2 * p + 1])
+                spots = (bzo[2 * p] + bzp[2 * p]) + (bzo[2 * p + 1] + bzp[2 * p + 1])
                 dx = tsr[0] - spots[0:1]
                 dy = tsr[1] - spots[1:2]
                 scaled = jnp.sqrt(dx * dx + dy * dy + 1e-06) * (3.0**0.5 / length_scale)
@@ -232,7 +233,7 @@
             rr[p, half, y] = value
             zb[o, z] = value
 
-    def forward(o):
+    def to_column(o):
         with jax.named_scope("z_wait"):
             await_bytes(zb.at[0, 0:7], rz_rec.at[o])
         with jax.named_scope("to_column"):
@@ -241,18 +242,25 @@
 
                 @pl.when(zz != y)
                 def _():
-                    push(zb.at[o, zz], rc.at[p, y], "cy", at_y(zz))
+                    push(zb.at[o, zz], rc.at[p, y], "cy", at_y(zz), cy_rec.at[o])
 
                 @pl.when(zz == y)
                 def _():
                     rc[p, y] = zb[o, zz]
 
+    def hand_over(o):
+        with jax.named_scope("hand_over"):
+            await_bytes(rc.at[0, 0:7], cy_rec.at[o])
+            there = rc.at[order_of(y)[o]]
+            push(there, there, "cp", partner, cp_rec.at[o])
+
+    def to_row(o):
         with jax.named_scope("r_wait"):
             await_bytes(rr.at[0, 0, 0:7], ry_rec.at[o])
         with jax.named_scope("to_row"):
             for d in (2, 1, 3):
                 there = rr.at[order[o], half]
-                push(there, there, "rx", at_x((x + d) % NX))
+                push(there, there, "rx", at_x((x + d) % NX), rx_rec.at[o])
 
     first_taking = 2 + 2 * core
     second_taking = 8 - 2 * core
@@ -268,20 +276,20 @@
 
     def factor_z():
         with jax.named_scope("factor_z"):
-            await_bytes(lzo.at[0, 0:7], rec.at[K["lz"]])
-            push(lzo.at[0], lzp.at[0], "lp", partner)
+            await_bytes(lzo.at[0:7], rec.at[K["lz"]])
+            push(lzo, lzp, "lp", partner)
 
     def sites_z():
         with jax.named_scope("sites_z"):
-            await_bytes(lzo.at[1, 0:7], rec.at[K["bz"]])
-            push(lzo.at[1], lzp.at[1], "bp", partner)
+            await_bytes(bzo.at[0:7], rec.at[K["bz"]])
+            push(bzo, bzp, "bp", partner)
 
     def factor_y():
         with jax.named_scope("factor_y"):
-            await_bytes(lzp.at[0], rec.at[K["lp"]])
+            await_bytes(lzp, rec.at[K["lp"]])
             low = lax.broadcasted_iota(jnp.int32, (8, 128), 1) < 64
             for q in range(4):
-                t0, t1 = (lzo[0, k] + lzp[0, k] for k in (2 * q, 2 * q + 1))
+                t0, t1 = (lzo[k] + lzp[k] for k in (2 * q, 2 * q + 1))
                 lt16[q, 0:8] = jnp.where(low, t0, pltpu.roll(t1, 64, 1))
                 lt16[q, 8:16] = jnp.where(low, pltpu.roll(t0, 64, 1), t1)
             lt[core, 0, y, x] = lt16[core]
@@ -289,7 +297,7 @@
 
             def along_y(slot):
                 here = lt.at[core, slot, y, x]
-                for d in FAR_FIRST:
+                for d in NEAR_FIRST:
                     push(here, here, f"ly{slot}", at_y((y + d) % NY))
 
             pl.when(first_in)(lambda: along_y(0))
@@ -310,7 +318,7 @@
 
             def along_x(k, slot, n):
                 part = lt.at[k, slot, 0:n, x]
-                for d in (2, 1, 3):
+                for d in (1, 3, 2):
                     push(part, part, f"lx{slot}", at_x((x + d) % NX))
 
             each_part(along_x)
@@ -399,12 +407,13 @@
         factor_x()
         for o in range(4):
             y_sum(o)
-        forward(0)
         factor_arrives()
         factor_pair()
-        forward(1)
-        forward(2)
-        forward(3)
+        for o in range(4):
+            to_column(o)
+            to_row(o)
+        for o in range(4):
+            hand_over(o)
         with jax.named_scope("inverse_wait"):
             await_bytes(wf, rec.at[K["w"]])
 
@@ -413,41 +422,41 @@
         factor_x()
         factor_arrives()
         inverse()
+        await_bytes(bzp, rec.at[K["bp"]])
 
     split_inverse()
 
-    with jax.named_scope("column_wait"):
-
-        @pl.when(takes)
-        def _():
-            await_bytes(rc.at[:, 0:7], rec.at[K["cy"]])
-            push(rc, rc, "cp", partner)
-
-    with jax.named_scope("row_wait"):
-
-        @pl.when(takes)
-        def _():
-            await_bytes(rr.at[:, 0], rec.at[K["rx"]])
-
-        @pl.when(rests)
-        def _():
-            await_bytes(rr, rec.at[K["rx"]])
-
-    with jax.named_scope("row_solve"):
-        solver = (wh[...], wl[...])
-        right = jnp.concatenate([rr[p].reshape(256, 128) for p in range(4)], axis=1)
-        vr = halves(dot3(halves(right), solver))
-        loads["pc"].wait()
-    with jax.named_scope("column_pair"):
-
-        @pl.when(rests)
-        def _():
-            await_bytes(rc, rec.at[K["cp"]])
-            await_bytes(lzp.at[1], rec.at[K["bp"]])
-
+    def solved(chunks, rights):
+        rows = [pl.ds(pl.multiple_of(128 * p, 128), 128) for p in chunks]
+        solver = [jnp.concatenate([ref[at] for at in rows], axis=0) for ref in (wh, wl)]
+        return dot3(halves(jnp.concatenate(rights, axis=1)), solver)
+
+    def row_part(turns):
+        with jax.named_scope("row_wait"):
+            for o in turns:
+                pl.when(takes)(lambda: await_bytes(rr.at[0, 0], rx_rec.at[o]))
+                pl.when(rests)(lambda: await_bytes(rr.at[0], rx_rec.at[o]))
+        with jax.named_scope("row_solve"):
+            chunks = [order[o] for o in turns]
+            return solved(chunks, [rr[p].reshape(256, 128) for p in chunks])
+
+    def column_part(turns):
+        with jax.named_scope("column_wait"):
+
+            @pl.when(rests)
+            def _():
+                for o in turns:
+                    await_bytes(rc.at[0], cp_rec.at[o])
+
+        with jax.named_scope("column_solve"):
+            chunks = [order_of(y)[o] for o in turns]
+            return solved(chunks, [rc[p].reshape(128, 128) for p in chunks])
+
+    vr = halves(row_part((0, 1, 2, 3)))
+    loads["pc"].wait()
+    acc[...] = column_part((0, 1, 2))
+    vc = acc[...] + column_part((3,))
     with jax.named_scope("update"):
-        right = jnp.concatenate([rc[p].reshape(128, 128) for p in range(4)], axis=1)
-        vc = dot3(halves(right), solver)
         cov_out[...] = pc[...] - dot3(vr, halves(vc), ((1,), (1,)))
         for p in range(4):
             vs[p] = vc[:, 128 * p : 128 * p + 128]
@@ -455,10 +464,10 @@
         v_out[...] = vs[4, pl.ds(pl.multiple_of(32 * (row % 4), 32), 32)]
 
     with jax.named_scope("drain"):
-        await_bytes(lzo.at[0, 0:7], send.at[K["lz"]])
-        await_bytes(lzo.at[1, 0:7], send.at[K["bz"]])
-        await_bytes(lzo.at[0], send.at[K["lp"]])
-        await_bytes(lzo.at[1], send.at[K["bp"]])
+        await_bytes(lzo.at[0:7], send.at[K["lz"]])
+        await_bytes(bzo.at[0:7], send.at[K["bz"]])
+        await_bytes(lzo, send.at[K["lp"]])
+        await_bytes(bzo, send.at[K["bp"]])
         pl.when(first_in)(lambda: await_bytes(lt.at[0, 0, 0:7, 0], send.at[K["ly0"]]))
         pl.when(second_in)(lambda: await_bytes(lt.at[0, 1, 0:7, 0], send.at[K["ly1"]]))
         each_part(lambda k, slot, n: await_bytes(lt.at[k, slot, 0:n, 0:3], send.at[K[f"lx{slot}"]]))
@@ -475,10 +484,10 @@
             await_bytes(xb.at[:, 0], send.at[K["ux"]])
             await_bytes(ub.at[:, 0:7], send.at[K["uy"]])
             await_bytes(zb.at[:, 0:7], send.at[K["rz"]])
+            await_bytes(rc.at[:, 0:7], send.at[K["cy"]])
+            await_bytes(rc, send.at[K["cp"]])
             await_bytes(zb.at[:, 0:7], send.at[K["ry"]])
             await_bytes(xb.at[:, 0:3], send.at[K["rx"]])
-            await_bytes(rc.at[:, 0:7], send.at[K["cy"]])
-            await_bytes(rc, send.at[K["cp"]])
 
         @pl.when(rests)
         def _():
@@ -499,8 +508,9 @@
         (4, NY, 16, 128),
         (NY, 2, 16, 128),
         (2, 16, 128),
-        (2, 8, 128),
-        (2, 8, 8, 128), (2, 8, 8, 128),
+        (8, 128), (2, 128),
+        (8, 8, 128), (8, 8, 128),
+        (8, 2, 128), (8, 2, 128),
         (4, 16, 128),
         (2, 2, 8, 4, 16, 128),
         (10, 128, 128),
@@ -509,6 +519,7 @@
         (4, 2, NY, 16, 128),
         (4, NZ, 16, 128),
         (4, NY, 16, 128),
+        (128, 512),
         (5, 128, 128),
     ]
     scratch = []
@@ -519,7 +530,7 @@
             scratch.append(pltpu.VMEM((512, 512), BF16))
         else:
             scratch.append(pltpu.VMEM(shape, F32))
-    counts = (len(LOADS), len(NAMES), len(NAMES), 8, 8, 4, 4, 4, 4)
+    counts = (len(LOADS), len(NAMES), len(NAMES), 8, 8, 4, 4, 4, 4, 4, 4, 4)
     scratch += [pltpu.SemaphoreType.DMA((n,)) for n in counts]
     return pl.pallas_call(
         kernel,

time: 50.9 us -> 50.2 us (0.986)
  Pallas kernels: 48.9 us -> 48.1 us
    pallas_call x1, Pallas kernels: 48.9 us -> 48.1 us  [local(): pl.pallas_call(kernel, out_shape=(pltpu.VMEM((32, 128), F32), pltpu.VMEM(...]
where the time goes in v4:
time: 50.2 us; the launch traced here: 50 us
  Pallas kernels  48.1 us (96%)
  local copies, waits for them, and re-layouts  1.26 us (3%)
  between operations  0.64 us (1%)
    pallas_call x1, Pallas kernels, local(): pl.pallas_call(kernel, out_shape=(pltpu.VMEM((32, 128), F32), pltpu.VMEM(...  48.1 us
    unnamed x2, local copies, waits for them, and re-layouts  1.26 us

profile of v4, /device:TPU:1, one launch (start us, length us, event | category | flops | bytes accessed | tf_op | source)
XLA Modules:
  0.0 50.0 jit_solution(10644826724252915549)
XLA Ops:
  0.6 48.1 %shard_map.77 = (f32[32,128]{1,0:T(8,128)S(1)}, f32[256,128]{1,0:T(8,128)S(1)}) custom-call(f32[2,32]{1,0:T(2,128)} %bs_in.1, f32[2,128]{1,0:T(2,128)} %ts_in.1, f32[16,32]{1,0:T(8,128)} %bitcast.1, f32[32,256]{1,0:T(8,128)} %a_in.1, f32[256,256]{1,0:T(8,128)} %s_in.1, f32[256,128]{1,0:T(8,128)} %pc_in.1), custom_call_target="tpu_custom_call" | custom-call | tf_op jit(solution)/shard_map/pallas_call | solution.py:535
  48.8 0.6 %copy.10 = f32[32,128]{1,0:T(8,128)} copy(f32[32,128]{1,0:T(8,128)S(1)} %get-tuple-element.2) | data formatting | bytes 32768
  49.4 0.7 %copy.11 = f32[256,128]{1,0:T(8,128)} copy(f32[256,128]{1,0:T(8,128)S(1)} %get-tuple-element.3) | data formatting | bytes 262144

commit v5 on v4

--- a/solution.py
+++ b/solution.py
@@ -407,9 +407,11 @@
         factor_x()
         for o in range(4):
             y_sum(o)
+        to_column(0)
+        to_row(0)
         factor_arrives()
         factor_pair()
-        for o in range(4):
+        for o in range(1, 4):
             to_column(o)
             to_row(o)
         for o in range(4):

time: 50.2 us -> 50.2 us (level)
  no operation moved by 1% of the time
where the time goes in v5:
time: 50.2 us; the launch traced here: 50 us
  Pallas kernels  48.1 us (96%)
  local copies, waits for them, and re-layouts  1.26 us (3%)
  between operations  0.64 us (1%)
    pallas_call x1, Pallas kernels, local(): pl.pallas_call(kernel, out_shape=(pltpu.VMEM((32, 128), F32), pltpu.VMEM(...  48.1 us
    unnamed x2, local copies, waits for them, and re-layouts  1.26 us

profile of v5, /device:TPU:1, one launch (start us, length us, event | category | flops | bytes accessed | tf_op | source)
XLA Modules:
  0.0 50.0 jit_solution(10083314626229167072)
XLA Ops:
  0.6 48.1 %shard_map.77 = (f32[32,128]{1,0:T(8,128)S(1)}, f32[256,128]{1,0:T(8,128)S(1)}) custom-call(f32[2,32]{1,0:T(2,128)} %bs_in.1, f32[2,128]{1,0:T(2,128)} %ts_in.1, f32[16,32]{1,0:T(8,128)} %bitcast.1, f32[32,256]{1,0:T(8,128)} %a_in.1, f32[256,256]{1,0:T(8,128)} %s_in.1, f32[256,128]{1,0:T(8,128)} %pc_in.1), custom_call_target="tpu_custom_call" | custom-call | tf_op jit(solution)/shard_map/pallas_call | solution.py:537
  48.8 0.6 %copy.10 = f32[32,128]{1,0:T(8,128)} copy(f32[32,128]{1,0:T(8,128)S(1)} %get-tuple-element.2) | data formatting | bytes 32768
  49.4 0.7 %copy.11 = f32[256,128]{1,0:T(8,128)} copy(f32[256,128]{1,0:T(8,128)S(1)} %get-tuple-element.3) | data formatting | bytes 262144
